TPU v7x, 128 devices: a whole 4x4x4 slice. The times are simulated.
128 devices in a mesh: dp: 2 (over x_hi), seq: 8 (over x_lo, y), tensor: 8 (over z, core).
Axes of the slice: x: 4 (x_hi: 2, x_lo: 2; x = x_hi * 2 + x_lo), y: 4, z: 4, core: 2. Of those that a mesh axis runs over, the one named last changes fastest.
Arguments:
- inputs: bfloat16 [8, 2048, 1024], P('dp', 'seq'), may hold values from -6 to 6
- w_qkv: bfloat16 [2, 1024, 3, 1024], P(None, ('dp', 'seq'), None, 'tensor'), may hold values from -0.1875 to 0.1875
- w_dense: bfloat16 [2, 1024, 1024], P(None, ('dp', 'seq'), 'tensor'), may hold values from -0.75 to 0.75
- w_fc1: bfloat16 [2, 1024, 4096], P(None, ('dp', 'seq'), 'tensor'), may hold values from -0.1875 to 0.1875
- w_fc2: bfloat16 [2, 1024, 4096], P(None, ('dp', 'seq'), 'tensor'), may hold values from -0.09375 to 0.09375
- norm_gain: bfloat16 [2, 2048], P(None, ('dp', 'seq')), may hold values from 0.5 to 1.5
- biases: bfloat16 [2, 11264], P(None, ('dp', 'seq')), may hold values from -1.75 to 1.75
- segment_ids: int32 [8, 2048], P('dp'), may hold values from 0 to 4, as said below
- cotangent: bfloat16 [8, 2048, 1024], P('dp', 'seq', 'tensor'), may hold values from -6 to 6
Outputs:
- block_out: bfloat16 [8, 2048, 1024], P('dp', 'seq')
- grad_inputs: float32 [8, 2048, 1024], P('dp', 'seq', 'tensor')
- grad_w_qkv: float32 [2, 1024, 3, 1024], P(None, ('dp', 'seq'), None, 'tensor')
- grad_w_dense: float32 [2, 1024, 1024], P(None, ('dp', 'seq'), 'tensor')
- grad_w_fc1: float32 [2, 1024, 4096], P(None, ('dp', 'seq'), 'tensor')
- grad_w_fc2: float32 [2, 1024, 4096], P(None, ('dp', 'seq'), 'tensor')
- grad_norm_gain: float32 [2, 2048], P(None, ('dp', 'seq'))
- grad_biases: float32 [2, 11264], P(None, ('dp', 'seq'))
Inputs may be any that keep to these rules, and one draw needn't show every extreme that they name: `segment_ids`: along each sequence the ids never fall, and the positions of one id are one document. Of each aligned block of 4 sequences exactly one is a single document; every other sequence ends with id 4.
All inputs are finite; a program needn't handle non-finite values.
Results may differ from a plain program's by a relative error of at most 0.025.
Values may be sent and summed in bfloat16 or wider, within the bound.
No kernel may reach another device: no remote copies, remote signals or barrier semaphores. Data moves between devices by JAX's collectives and lax.ppermute only.
A program may use at most 256 MiB of HBM per device.

v0:
```python
import math

import jax
import jax.numpy as jnp
from jax import lax
from jax.sharding import PartitionSpec as P

D = 1024
FF = 4096
HEAD = 64
ROT = 16
LAYERS = 2
MICRO = 2


epsilon = 1e-05


def side_by_side(arrays, axis, dim, along):
    columns = [a.reshape(*a.shape[:along], -1) for a in arrays]
    both = jnp.concatenate(columns, axis=along)
    filled, at, finished = (lax.all_gather(both, axis, axis=dim, tiled=True), 0, [])
    for a, column in zip(arrays, columns):
        slab = filled[..., at : at + column.shape[along]]
        finished.append(slab.reshape(*slab.shape[:along], *a.shape[along:]))
        at += column.shape[along]
    return tuple(finished)


def side_by_side_2(arrays, axis, dim, along):
    ends, at = ([], 0)
    for a in arrays[:-1]:
        at += a.shape[along]
        ends.append(at)
    both = jnp.concatenate(arrays, axis=along)
    return tuple(jnp.split(lax.all_gather(both, axis, axis=dim, tiled=True), ends, axis=along))


def padded_to(lines, size):
    spare = -len(lines) % size
    return jnp.pad(lines, [(0, spare)] + [(0, 0)] * (lines.ndim - 1))


def total_of(shard, axis):
    lines = shard.reshape(-1, *shard.shape[1:][-1:])
    padded = padded_to(lines, lax.axis_size(axis))
    own = lax.psum_scatter(padded, axis, scatter_dimension=0, tiled=True)
    whole = lax.all_gather(own, axis, axis=0, tiled=True)
    return whole[: len(lines)].reshape(shard.shape)


def sent_to_all(shard, axis):
    copies = jnp.broadcast_to(shard, (lax.axis_size(axis), *shard.shape))
    return lax.all_to_all(copies, axis, split_axis=0, concat_axis=0, tiled=True)


def laid_out(tiles, dim):
    dims = list(tiles.shape[1:])
    dims[dim] *= tiles.shape[0]
    return jnp.moveaxis(tiles, 0, dim).reshape(dims)


def collect(shard, axis, dim):
    tiles = sent_to_all(shard, axis)
    return laid_out(tiles, dim)


def side_by_side_3(arrays, axis, dim, along):
    ends, at = ([], 0)
    for a in arrays[:-1]:
        at += a.shape[along]
        ends.append(at)
    both = jnp.concatenate(arrays, axis=along)
    return tuple(
        jnp.split(lax.psum_scatter(both, axis, scatter_dimension=dim, tiled=True), ends, axis=along)
    )


def in_blocks(shard, dim, size):
    before, after = (shard.shape[:dim], shard.shape[dim + 1 :])
    return jnp.moveaxis(shard.reshape(*before, size, -1, *after), dim, 0)


def sent_and_summed(shard, axis, dim):
    size = lax.axis_size(axis)
    tiles = lax.all_to_all(in_blocks(shard, dim, size), axis, 0, 0, tiled=True)
    return jnp.sum(tiles.astype(jnp.float32), axis=0)


def sent_together(arrays, axis, dim, along):
    widths = [math.prod(a.shape[along:]) for a in arrays]
    both = jnp.concatenate(
        [a.reshape(*a.shape[:along], w) for a, w in zip(arrays, widths)], axis=along
    )
    filled = lax.psum_scatter(both, axis, scatter_dimension=dim, tiled=True)
    tiles = jnp.split(filled, [sum(widths[:k]) for k in range(1, len(widths))], axis=along)
    return tuple(
        (b.reshape(*filled.shape[:along], *a.shape[along:]) for a, b in zip(arrays, tiles))
    )


def of_everyone(shard, axis):
    return sent_to_all(shard, axis).sum(axis=0)


def in_one(arrays, axis):
    line, at, finished = (jnp.concatenate([a.reshape(-1) for a in arrays]), 0, [])
    subtotal = of_everyone(line, axis)
    for a in arrays:
        finished.append(subtotal[at : at + a.size].reshape(a.shape))
        at += a.size
    return tuple(finished)


def layer_norm(values, gain_vec, shift_vec):
    centred = values - jnp.mean(values, axis=-1, keepdims=True)
    variance = jnp.mean(centred * centred, axis=-1, keepdims=True)
    return centred * lax.rsqrt(variance + epsilon) * gain_vec + shift_vec


def two_norms(residual, gain_vec, shift_vec):
    half_width = gain_vec.shape[0] // 2
    return (
        layer_norm(residual, gain_vec[:half_width], shift_vec[:half_width]),
        layer_norm(residual, gain_vec[half_width:], shift_vec[half_width:]),
    )


def rotate(values, places):
    half_rot = ROT // 2
    inverse = 10000.0 ** (-jnp.arange(half_rot, dtype=jnp.float32) * 2.0 / ROT)
    angles = places.astype(jnp.float32)[..., None] * inverse
    angles = jnp.concatenate([angles, angles], axis=-1)[..., None, :]
    cosine = jnp.cos(angles)
    sines = jnp.sin(angles)
    turned_part = values[..., :ROT]
    swapped = jnp.concatenate([-turned_part[..., half_rot:], turned_part[..., :half_rot]], axis=-1)
    return jnp.concatenate([turned_part * cosine + swapped * sines, values[..., ROT:]], axis=-1)


def gelu_exact(values):
    return jax.nn.gelu(values, approximate=False)


def shards(inputs, w_qkv, w_dense, w_fc1, w_fc2, norm_gain, biases, segment_ids, cotangent):
    tensor_rank = lax.axis_index("tensor")
    seq_rank = lax.axis_index("seq")
    local_len = inputs.shape[1]
    full_len = segment_ids.shape[1]
    per_micro = inputs.shape[0] // MICRO
    head_cols = w_qkv.shape[3]
    hidden_cols = w_fc1.shape[2]
    column_count = cotangent.shape[2]
    heads_here = head_cols // HEAD
    head_shape = (per_micro, local_len, heads_here, HEAD)
    full_shape = (per_micro, full_len, heads_here, HEAD)
    scaling = HEAD ** (-0.5)
    query_rows = seq_rank * local_len + jnp.arange(local_len, dtype=jnp.int32)
    key_rows = jnp.arange(full_len, dtype=jnp.int32)

    def gather_layer(layer_id):
        return (
            *side_by_side(
                (w_qkv[layer_id], w_dense[layer_id], w_fc1[layer_id], w_fc2[layer_id]),
                ("dp", "seq"),
                0,
                1,
            ),
            lax.all_gather(norm_gain[layer_id], ("dp", "seq"), axis=0, tiled=True),
            lax.all_gather(biases[layer_id], ("dp", "seq"), axis=0, tiled=True),
        )

    def unpack(gathered):
        qkv_weight, dense_weight, fc1_weight, fc2_weight, gain_vec, bias_vec = gathered
        gain_vec = gain_vec.astype(jnp.float32)
        bias_vec = bias_vec.astype(jnp.float32)
        qkv_bias = lax.dynamic_slice_in_dim(
            bias_vec[2 * D : 5 * D].reshape(3, D), tensor_rank * head_cols, head_cols, 1
        )
        fc1_bias = lax.dynamic_slice_in_dim(
            bias_vec[6 * D : 6 * D + FF], tensor_rank * hidden_cols, hidden_cols, 0
        )
        outer_bias = bias_vec[5 * D : 6 * D] + bias_vec[6 * D + FF :]
        return (
            qkv_weight,
            dense_weight,
            fc1_weight,
            fc2_weight,
            gain_vec,
            bias_vec[: 2 * D],
            qkv_bias,
            fc1_bias,
            outer_bias,
        )

    def masks_for(segments):
        own_ids = lax.dynamic_slice_in_dim(segments, seq_rank * local_len, local_len, 1)
        earlier = jnp.sum((segments[:, None, :] < own_ids[:, :, None]).astype(jnp.int32), axis=-1)
        places = query_rows[None, :] - earlier
        allowed = (own_ids[:, :, None] == segments[:, None, :]) & (
            key_rows[None, None, :] <= query_rows[None, :, None]
        )
        return (places, allowed[:, None])

    def score_block(queries, keys_heads, allowed):
        scores = (
            jnp.einsum("bqhe,bkhe->bhqk", queries, keys_heads, preferred_element_type=jnp.float32)
            * scaling
        )
        return jnp.where(allowed, scores, -1e30)

    residuals = [
        inputs[micro_id * per_micro : (micro_id + 1) * per_micro].astype(jnp.float32)
        for micro_id in range(MICRO)
    ]
    stored = []
    for layer_id in range(LAYERS):
        layer_store = []
        for micro_id in range(MICRO):
            current = gather_layer(layer_id)
            (
                qkv_weight,
                dense_weight,
                fc1_weight,
                fc2_weight,
                gain_vec,
                shift_vec,
                qkv_bias,
                fc1_bias,
                outer_bias,
            ) = unpack(current)
            residual = residuals[micro_id]
            segments = segment_ids[micro_id * per_micro : (micro_id + 1) * per_micro]
            places, allowed = masks_for(segments)
            normed_one, normed_two = two_norms(residual, gain_vec, shift_vec)
            normed_one = normed_one.astype(jnp.bfloat16)
            normed_two = normed_two.astype(jnp.bfloat16)
            projected = (
                jnp.einsum(
                    "bsd,dke->bske", normed_one, qkv_weight, preferred_element_type=jnp.float32
                )
                + qkv_bias
            )
            queries = rotate(projected[:, :, 0].reshape(head_shape), places).astype(jnp.bfloat16)
            keys_own = rotate(projected[:, :, 1].reshape(head_shape), places).astype(jnp.bfloat16)
            keys_own = keys_own.reshape(per_micro, local_len, head_cols)
            values_own = projected[:, :, 2].astype(jnp.bfloat16)
            keys_all, values_all = side_by_side_2((keys_own, values_own), "seq", 1, 0)
            scores = score_block(queries, keys_all.reshape(full_shape), allowed)
            largest = jnp.max(scores, axis=-1, keepdims=True)
            exponent = jnp.exp(scores - largest)
            totals = jnp.sum(exponent, axis=-1, keepdims=True)
            attn_probs = (exponent / totals).astype(jnp.bfloat16)
            attended = jnp.einsum(
                "bhqk,bkhe->bqhe",
                attn_probs,
                values_all.reshape(full_shape),
                preferred_element_type=jnp.float32,
            )
            attended = attended.reshape(per_micro, local_len, head_cols).astype(jnp.bfloat16)
            pre_act = (
                jnp.einsum(
                    "bsd,df->bsf", normed_two, fc1_weight, preferred_element_type=jnp.float32
                )
                + fc1_bias
            )
            activated = gelu_exact(pre_act).astype(jnp.bfloat16)
            partial_out = jnp.einsum(
                "bsw,ow->bso", attended, dense_weight, preferred_element_type=jnp.float32
            )
            partial_out = partial_out + jnp.einsum(
                "bsf,of->bso", activated, fc2_weight, preferred_element_type=jnp.float32
            )
            summed = total_of(partial_out.astype(jnp.bfloat16), "tensor").astype(jnp.float32)
            residuals[micro_id] = residual + (summed + outer_bias)
            layer_store.append(
                (
                    residual,
                    queries,
                    keys_own,
                    values_own,
                    attended,
                    largest + jnp.log(totals),
                    pre_act,
                )
            )
        stored.append(layer_store)
    block_out = jnp.concatenate(residuals, axis=0).astype(jnp.bfloat16)
    grad_streams = [
        cotangent[micro_id * per_micro : (micro_id + 1) * per_micro].astype(jnp.float32)
        for micro_id in range(MICRO)
    ]
    layer_grads = []
    for layer_id in reversed(range(LAYERS)):
        grad_qkv_sum = jnp.zeros((D, 3, head_cols), jnp.float32)
        grad_dense_sum = jnp.zeros((D, head_cols), jnp.float32)
        grad_fc1_sum = jnp.zeros((D, hidden_cols), jnp.float32)
        grad_fc2_sum = jnp.zeros((D, hidden_cols), jnp.float32)
        grad_gain_sum = jnp.zeros((2 * D,), jnp.float32)
        grad_bias_sum = jnp.zeros((7 * D + FF,), jnp.float32)
        for micro_id in range(MICRO):
            current = gather_layer(layer_id)
            (
                qkv_weight,
                dense_weight,
                fc1_weight,
                fc2_weight,
                gain_vec,
                shift_vec,
                qkv_bias,
                fc1_bias,
                outer_bias,
            ) = unpack(current)
            residual, queries, keys_own, values_own, attended, log_total, pre_act = stored[
                layer_id
            ][micro_id]
            segments = segment_ids[micro_id * per_micro : (micro_id + 1) * per_micro]
            places, allowed = masks_for(segments)
            grad_cols = grad_streams[micro_id]
            cols_low = grad_cols.astype(jnp.bfloat16)
            grad_low = collect(cols_low, "tensor", 2)
            col_sums = jnp.sum(cols_low, axis=(0, 1), dtype=jnp.float32)
            gelu_value, gelu_back = jax.vjp(gelu_exact, pre_act)
            activated = gelu_value.astype(jnp.bfloat16)
            grad_dense_sum = grad_dense_sum + jnp.einsum(
                "bso,bsw->ow", grad_low, attended, preferred_element_type=jnp.float32
            )
            grad_fc2_sum = grad_fc2_sum + jnp.einsum(
                "bso,bsf->of", grad_low, activated, preferred_element_type=jnp.float32
            )
            grad_att = jnp.einsum(
                "bso,ow->bsw", grad_low, dense_weight, preferred_element_type=jnp.float32
            )
            grad_act = jnp.einsum(
                "bso,of->bsf", grad_low, fc2_weight, preferred_element_type=jnp.float32
            )
            grad_pre = gelu_back(grad_act)[0].astype(jnp.bfloat16)
            normed_values, norm_back = jax.vjp(two_norms, residual, gain_vec, shift_vec)
            normed_one = normed_values[0].astype(jnp.bfloat16)
            normed_two = normed_values[1].astype(jnp.bfloat16)
            grad_fc1_sum = grad_fc1_sum + jnp.einsum(
                "bsd,bsf->df", normed_two, grad_pre, preferred_element_type=jnp.float32
            )
            pre_sums = jnp.sum(grad_pre, axis=(0, 1), dtype=jnp.float32)
            grad_two = jnp.einsum(
                "bsf,df->bsd", grad_pre, fc1_weight, preferred_element_type=jnp.float32
            )
            grad_heads = grad_att.astype(jnp.bfloat16).reshape(head_shape)
            keys_all, values_all = side_by_side_2((keys_own, values_own), "seq", 1, 0)
            keys_heads = keys_all.reshape(full_shape)
            scores = score_block(queries, keys_heads, allowed)
            attn_probs = jnp.exp(scores - log_total)
            grad_probs = jnp.einsum(
                "bqhe,bkhe->bhqk",
                grad_heads,
                values_all.reshape(full_shape),
                preferred_element_type=jnp.float32,
            )
            row_dot = jnp.sum(attn_probs * grad_probs, axis=-1, keepdims=True)
            grad_scores = (attn_probs * (grad_probs - row_dot)).astype(jnp.bfloat16)
            grad_queries = (
                jnp.einsum(
                    "bhqk,bkhe->bqhe", grad_scores, keys_heads, preferred_element_type=jnp.float32
                )
                * scaling
            )
            grad_values_all = jnp.einsum(
                "bhqk,bqhe->bkhe",
                attn_probs.astype(jnp.bfloat16),
                grad_heads,
                preferred_element_type=jnp.float32,
            )
            grad_keys_all = (
                jnp.einsum(
                    "bhqk,bqhe->bkhe", grad_scores, queries, preferred_element_type=jnp.float32
                )
                * scaling
            )
            grad_keys, grad_values = tuple(
                (
                    part.astype(jnp.float32)
                    for part in side_by_side_3(
                        (
                            grad_keys_all.reshape(per_micro, full_len, head_cols).astype(
                                jnp.bfloat16
                            ),
                            grad_values_all.reshape(per_micro, full_len, head_cols).astype(
                                jnp.bfloat16
                            ),
                        ),
                        "seq",
                        1,
                        0,
                    )
                )
            )

            def turn(values):
                return rotate(values, places)

            _, turn_back = jax.vjp(turn, jnp.zeros(head_shape, jnp.float32))
            grad_q_pre = turn_back(grad_queries)[0].reshape(per_micro, local_len, head_cols)
            grad_k_pre = turn_back(grad_keys.reshape(head_shape))[0].reshape(
                per_micro, local_len, head_cols
            )
            grad_proj = jnp.stack([grad_q_pre, grad_k_pre, grad_values], axis=2).astype(
                jnp.bfloat16
            )
            grad_qkv_sum = grad_qkv_sum + jnp.einsum(
                "bsd,bske->dke", normed_one, grad_proj, preferred_element_type=jnp.float32
            )
            proj_sums = jnp.sum(grad_proj, axis=(0, 1), dtype=jnp.float32)
            grad_one = jnp.einsum(
                "bske,dke->bsd", grad_proj, qkv_weight, preferred_element_type=jnp.float32
            )
            grad_resid, grad_gain, grad_shift = norm_back((grad_one, grad_two))
            share_cols = sent_and_summed(grad_resid.astype(jnp.bfloat16), "tensor", 2)
            grad_streams[micro_id] = grad_cols + share_cols
            grad_gain_sum = grad_gain_sum + grad_gain
            proj_full = lax.dynamic_update_slice(
                jnp.zeros((3, D), jnp.float32), proj_sums, (jnp.int32(0), tensor_rank * head_cols)
            )
            cols_full = lax.dynamic_update_slice_in_dim(
                jnp.zeros((D,), jnp.float32), col_sums, tensor_rank * column_count, 0
            )
            fc1_full = lax.dynamic_update_slice_in_dim(
                jnp.zeros((FF,), jnp.float32), pre_sums, tensor_rank * hidden_cols, 0
            )
            grad_bias_sum = grad_bias_sum + jnp.concatenate(
                [grad_shift, proj_full.reshape(3 * D), cols_full, fc1_full, cols_full]
            )
        shares = (
            *tuple(
                (
                    part.astype(jnp.float32)
                    for part in sent_together(
                        (
                            grad_qkv_sum.astype(jnp.bfloat16),
                            grad_dense_sum.astype(jnp.bfloat16),
                            grad_fc1_sum.astype(jnp.bfloat16),
                            grad_fc2_sum.astype(jnp.bfloat16),
                        ),
                        ("dp", "seq"),
                        0,
                        1,
                    )
                )
            ),
            lax.psum_scatter(
                grad_gain_sum.astype(jnp.bfloat16), ("dp", "seq"), scatter_dimension=0, tiled=True
            ).astype(jnp.float32),
            lax.psum_scatter(
                grad_bias_sum.astype(jnp.bfloat16), ("dp", "seq"), scatter_dimension=0, tiled=True
            ).astype(jnp.float32),
        )
        gain_share, bias_share = in_one((shares[4], shares[5]), "tensor")
        layer_grads.append((shares[0], shares[1], shares[2], shares[3], gain_share, bias_share))
    layer_grads = layer_grads[::-1]
    grad_inputs = jnp.concatenate(grad_streams, axis=0)
    stacked = [
        jnp.stack([entry[position] for entry in layer_grads], axis=0) for position in range(6)
    ]
    return (
        block_out,
        grad_inputs,
        stacked[0],
        stacked[1],
        stacked[2],
        stacked[3],
        stacked[4],
        stacked[5],
    )


def solution(mesh):
    in_specs = (
        P("dp", "seq", None),
        P(None, ("dp", "seq"), None, "tensor"),
        P(None, ("dp", "seq"), "tensor"),
        P(None, ("dp", "seq"), "tensor"),
        P(None, ("dp", "seq"), "tensor"),
        P(None, ("dp", "seq")),
        P(None, ("dp", "seq")),
        P("dp", None),
        P("dp", "seq", "tensor"),
    )
    out_specs = (
        P("dp", "seq", None),
        P("dp", "seq", "tensor"),
        P(None, ("dp", "seq"), None, "tensor"),
        P(None, ("dp", "seq"), "tensor"),
        P(None, ("dp", "seq"), "tensor"),
        P(None, ("dp", "seq"), "tensor"),
        P(None, ("dp", "seq")),
        P(None, ("dp", "seq")),
    )
    return jax.shard_map(shards, mesh=mesh, in_specs=in_specs, out_specs=out_specs, check_vma=False)
```

profile of v0, /device:TPU:0, one launch (start us, length us, event | category | flops | bytes accessed | tf_op | source)
XLA Modules:
  0.0 1018.0 jit_solution(3916229171390356951)
XLA Ops:
  15.9 75.1 %all-reduce.55 = (bf16[11264]{0:T(1024)(128)(2,1)S(1)}, bf16[11264]{0:T(1024)(128)(2,1)S(1)}) all-reduce(bf16[11264]{0:T(1024)(128)(2,1)S(1)} %dynamic-update-slice.1, bf16[11264]{0:T(1024)(128)(2,1)S(1)} %dynamic-update-slice), channel_id=5, replica_groups=mesh['dp'=2,'seq'=8,'tensor'=8] {'dp','seq'}, use_global_device_ids=true, to_apply=%add.49 | all-reduce | flops 22528 | bytes 90112
  93.5 17.0 %all-gather = bf16[1,2048]{1,0:T(2,128)(2,1)S(1)} all-gather(bf16[1,128]{1,0:T(2,128)(2,1)S(1)} %get-tuple-element.272), channel_id=2, replica_groups=mesh['dp'=2,'seq'=8,'tensor'=8] {'dp','seq'}, dimensions={1}, use_global_device_ids=true | all-gather | bytes 4352 | tf_op jit(solution)/shard_map/all_gather | solution.py:169
  145.0 24.7 %all-gather.27.cloned.1.call-done = bf16[4,2048,128]{1,2,0:T(8,128)(2,1)} async-done(((bf16[4,256,128]{1,2,0:T(8,128)(2,1)}), bf16[4,2048,128]{1,2,0:T(8,128)(2,1)}) %all-gather.27.cloned.1.call-update) | async-done | bytes 2097168 | tf_op jit(solution)/shard_map/all_gather | solution.py:36
  181.5 36.8 %all-gather.17.cloned.1.call-done = bf16[4,2048,128]{1,2,0:T(8,128)(2,1)} async-done(((bf16[4,256,128]{1,2,0:T(8,128)(2,1)}), bf16[4,2048,128]{1,2,0:T(8,128)(2,1)}) %all-gather.17.cloned.1.call-update) | async-done | bytes 2097168 | tf_op jit(solution)/shard_map/all_gather | solution.py:36
  231.0 22.8 %reduce-scatter.19.cloned.1.call-done = bf16[64,1024]{1,0:T(8,128)(2,1)} async-done(((bf16[512,1024]{1,0:T(8,128)(2,1)}), bf16[64,1024]{1,0:T(8,128)(2,1)}) %reduce-scatter.19.cloned.1.call-update) | async-done | bytes 131088 | tf_op jit(solution)/shard_map/reduce_scatter | solution.py:47
  253.9 33.5 %reduce-scatter.15.cloned.1.call-done = bf16[64,1024]{1,0:T(8,128)(2,1)} async-done(((bf16[512,1024]{1,0:T(8,128)(2,1)}), bf16[64,1024]{1,0:T(8,128)(2,1)}) %reduce-scatter.15.cloned.1.call-update) | async-done | bytes 131088 | tf_op jit(solution)/shard_map/reduce_scatter | solution.py:47
  288.7 4.2 all-to-all-start
  293.0 20.6 %all-gather.2 = bf16[1,2048]{1,0:T(2,128)(2,1)S(1)} all-gather(bf16[1,128]{1,0:T(2,128)(2,1)S(1)} %copy-done.245), channel_id=4, replica_groups=mesh['dp'=2,'seq'=8,'tensor'=8] {'dp','seq'}, dimensions={1}, use_global_device_ids=true | all-gather | bytes 4352 | tf_op jit(solution)/shard_map/all_gather | solution.py:169
  314.9 21.6 %all-gather.21.cloned.1.call-done = bf16[1024,1536]{1,0:T(8,128)(2,1)} async-done(((bf16[64,1536]{1,0:T(8,128)(2,1)}), bf16[1024,1536]{1,0:T(8,128)(2,1)}) %all-gather.21.cloned.1.call-update) | async-done | bytes 3145744 | tf_op jit(solution)/shard_map/all_gather | solution.py:22
  338.9 22.0 %all-gather.29.cloned.1.call-done = bf16[512,1024]{1,0:T(8,128)(2,1)} async-done(((bf16[64,1024]{1,0:T(8,128)(2,1)}), bf16[512,1024]{1,0:T(8,128)(2,1)}) %all-gather.29.cloned.1.call-update) | async-done | bytes 1048592 | tf_op jit(solution)/shard_map/all_gather | solution.py:48
  360.8 25.2 %all-gather.19.cloned.1.call-done = bf16[512,1024]{1,0:T(8,128)(2,1)} async-done(((bf16[64,1024]{1,0:T(8,128)(2,1)}), bf16[512,1024]{1,0:T(8,128)(2,1)}) %all-gather.19.cloned.1.call-update) | async-done | bytes 1048592 | tf_op jit(solution)/shard_map/all_gather | solution.py:48
  403.1 11.9 %all-to-all-done.4 = bf16[8,2,256,128]{3,2,1,0:T(8,128)(2,1)S(1)} async-done(((bf16[8,2,256,128]{3,2,1,0:T(8,128)(2,1)}), bf16[8,2,256,128]{3,2,1,0:T(8,128)(2,1)S(1)}, u32[]{:S(2)}, u32[]{:S(2)}) %all-to-all-start.4) | async-done | bytes 1048608 | tf_op jit(solution)/shard_map/all_to_all | solution.py:54
  421.2 4.7 fusion.211
  425.9 14.0 %all-gather.23.cloned.1.call-done = bf16[4,2048,128]{1,2,0:T(8,128)(2,1)} async-done(((bf16[4,256,128]{1,2,0:T(8,128)(2,1)}), bf16[4,2048,128]{1,2,0:T(8,128)(2,1)}) %all-gather.23.cloned.1.call-update) | async-done | bytes 2097168 | tf_op jit(solution)/shard_map/all_gather | solution.py:36
  452.8 5.1 multiply_reduce_fusion.3
  468.9 19.5 %all-gather.31.cloned.1.call-done = bf16[4,2048,128]{1,2,0:T(8,128)(2,1)} async-done(((bf16[4,256,128]{1,2,0:T(8,128)(2,1)}), bf16[4,2048,128]{1,2,0:T(8,128)(2,1)}) %all-gather.31.cloned.1.call-update) | async-done | bytes 2097168 | tf_op jit(solution)/shard_map/all_gather | solution.py:36
  501.3 5.1 multiply_reduce_fusion.1
  518.2 4.1 multiply_convert_fusion.6
  542.1 35.9 %reduce-scatter.27.cloned.1.call-done = bf16[4,256,128]{2,1,0:T(8,128)(2,1)} async-done(((bf16[4,2048,128]{2,1,0:T(8,128)(2,1)}), bf16[4,256,128]{2,1,0:T(8,128)(2,1)}) %reduce-scatter.27.cloned.1.call-update) | async-done | bytes 262160 | tf_op jit(solution)/shard_map/reduce_scatter | solution.py:75
  600.9 4.1 multiply_reduce_fusion.5
  608.7 4.6 all-to-all-start.1
  614.6 14.8 %all-to-all-done.1 = bf16[8,2,256,128]{3,2,1,0:T(8,128)(2,1)} async-done(((bf16[8,2,256,128]{3,2,1,0:T(8,128)(2,1)}), bf16[8,2,256,128]{3,2,1,0:T(8,128)(2,1)}, u32[]{:S(2)}, u32[]{:S(2)}) %all-to-all-start.1) | async-done | bytes 1048608 | tf_op jit(solution)/shard_map/all_to_all | solution.py:86
  633.0 5.5 fusion.106
  642.8 6.1 all-to-all-done.5
  653.1 3.6 all-to-all-start.6
  657.2 5.5 fusion.104
  665.5 9.2 all-to-all-done.6
  676.4 5.9 fusion.57
  684.6 5.8 multiply_reduce_fusion
  690.4 4.5 multiply_convert_fusion
  709.0 15.0 %all-to-all-done.2 = bf16[8,2,256,128]{3,2,1,0:T(8,128)(2,1)S(1)} async-done(((bf16[8,2,256,128]{3,2,1,0:T(8,128)(2,1)}), bf16[8,2,256,128]{3,2,1,0:T(8,128)(2,1)S(1)}, u32[]{:S(2)}, u32[]{:S(2)}) %all-to-all-start.2) | async-done | bytes 1048608 | tf_op jit(solution)/shard_map/all_to_all | solution.py:54
  725.6 6.0 fusion.51
  734.0 5.7 multiply_reduce_fusion.2
  739.7 4.5 multiply_convert_fusion.2
  783.6 3.7 fusion.100
  806.5 3.7 fusion.85
  847.2 4.8 copy.356
  853.6 4.7 fusion.74
  859.1 5.3 fusion.65
  864.5 72.1 %all-reduce.54 = (bf16[11264]{0:T(1024)(128)(2,1)S(1)}, bf16[2048]{0:T(1024)(128)(2,1)S(1)}, bf16[11264]{0:T(1024)(128)(2,1)S(1)}, bf16[2048]{0:T(1024)(128)(2,1)S(1)}) all-reduce(bf16[11264]{0:T(1024)(128)(2,1)S(1)} %copy-done.141, ...), channel_id=19, replica_groups=mesh['dp'=2,'seq'=8,'tensor'=8] {'dp','seq'}, use_global_device_ids=true, to_apply=%region_84.85.clone | all-reduce | flops 26624 | bytes 106496
  941.0 3.8 bitcast_bitcast_fusion
  950.3 5.3 all-to-all-done.8
  955.6 4.3 all-to-all-start.7
  960.0 4.5 fusion.81
  967.3 8.5 all-to-all-done.7
  975.8 3.6 all-to-all-start.3
  985.1 10.1 all-to-all-done.3
  996.3 8.0 reduce-scatter.31.cloned.1.call-done
  (937 shorter events, 350.6 us)
Async XLA Ops:
  7.2 106.1 %copy-start.4 = (bf16[4,256,1024]{2,1,0:T(8,128)(2,1)S(1)}, bf16[4,256,1024]{2,1,0:T(8,128)(2,1)}, u32[]{:S(2)}) copy-start(bf16[4,256,1024]{2,1,0:T(8,128)(2,1)} %param.9) | copy-start | bytes 6291460
  7.2 109.5 %all-gather.15.cloned.1.call-start = ((), (), s32[]{:S(2)}) async-start(), calls=%async_computation.20 | async-start | bytes 3342336 | tf_op jit(solution)/shard_map/all_gather | solution.py:22
  12.5 157.2 %all-gather.27.cloned.1.call-start = ((), (), s32[]{:S(2)}) async-start(), calls=%async_computation.28 | async-start | bytes 2359296 | tf_op jit(solution)/shard_map/all_gather | solution.py:36
  113.3 306.6 %copy-start.104 = (f32[2,256,16]{1,2,0:T(8,128)}, f32[2,256,16]{1,2,0:T(8,128)S(1)}, u32[]{:S(2)}) copy-start(f32[2,256,16]{1,2,0:T(8,128)S(1)} %get-tuple-element.252) | copy-start | bytes 98308
  113.3 306.6 %copy-start.106 = (f32[2,256,16]{1,2,0:T(8,128)}, f32[2,256,16]{1,2,0:T(8,128)S(1)}, u32[]{:S(2)}) copy-start(f32[2,256,16]{1,2,0:T(8,128)S(1)} %get-tuple-element.251) | copy-start | bytes 98308
  116.7 271.8 %copy-start.142 = (f32[1,1024]{1,0:T(1,128)}, f32[1,1024]{1,0:T(1,128)S(1)}, u32[]{:S(2)}) copy-start(f32[1,1024]{1,0:T(1,128)S(1)} %get-tuple-element.228) | copy-start | bytes 12292
  122.6 95.8 %all-gather.17.cloned.1.call-start = ((), (), s32[]{:S(2)}) async-start(), calls=%async_computation.21 | async-start | bytes 2359296 | tf_op jit(solution)/shard_map/all_gather | solution.py:36
  123.6 269.4 %copy-start.107 = (f32[2,256,16]{1,2,0:T(8,128)}, f32[2,256,16]{1,2,0:T(8,128)S(1)}, u32[]{:S(2)}) copy-start(f32[2,256,16]{1,2,0:T(8,128)S(1)} %get-tuple-element.253) | copy-start | bytes 98308
  123.6 417.8 %copy-start.105 = (f32[2,256,16]{1,2,0:T(8,128)}, f32[2,256,16]{1,2,0:T(8,128)S(1)}, u32[]{:S(2)}) copy-start(f32[2,256,16]{1,2,0:T(8,128)S(1)} %get-tuple-element.254) | copy-start | bytes 98308
  131.1 122.7 %reduce-scatter.19.cloned.1.call-start = ((), (), s32[]{:S(2)}) async-start(), calls=%async_computation.29 | async-start | bytes 1179648 | tf_op jit(solution)/shard_map/reduce_scatter | solution.py:47
  138.0 90.2 %copy-start.41 = (bf16[2,256,512]{2,1,0:T(8,128)(2,1)}, bf16[2,256,512]{2,1,0:T(8,128)(2,1)S(1)}, u32[]{:S(2)}) copy-start(bf16[2,256,512]{2,1,0:T(8,128)(2,1)S(1)} %get-tuple-element.134) | copy-start | bytes 1572868
  144.9 75.2 %copy-start.122 = (bf16[2,256,2,48]{1,3,2,0:T(8,128)(2,1)}, bf16[2,256,2,48]{1,3,2,0:T(8,128)(2,1)S(1)}, u32[]{:S(2)}) copy-start(bf16[2,256,2,48]{1,3,2,0:T(8,128)(2,1)S(1)} %slice.786) | copy-start | bytes 294916
  181.3 38.9 %copy-start.136 = (bf16[2,256,2,16]{1,3,2,0:T(8,128)(2,1)S(1)}, bf16[2,256,2,16]{1,3,2,0:T(8,128)(2,1)}, u32[]{:S(2)}) copy-start(bf16[2,256,2,16]{1,3,2,0:T(8,128)(2,1)} %get-tuple-element.223) | copy-start | bytes 98308
  181.3 106.2 %reduce-scatter.15.cloned.1.call-start = ((), (), s32[]{:S(2)}) async-start(), calls=%async_computation.22 | async-start | bytes 1179648 | tf_op jit(solution)/shard_map/reduce_scatter | solution.py:47
  230.0 57.5 %copy-start.66 = (bf16[4,256,128]{2,1,0:T(8,128)(2,1)S(1)}, bf16[4,256,128]{2,1,0:T(8,128)(2,1)}, u32[]{:S(2)}) copy-start(bf16[4,256,128]{2,1,0:T(8,128)(2,1)} %param.17) | copy-start | bytes 786436
  230.0 106.5 %all-gather.21.cloned.1.call-start = ((), (), s32[]{:S(2)}) async-start(), calls=%async_computation.24 | async-start | bytes 3342336 | tf_op jit(solution)/shard_map/all_gather | solution.py:22
  230.9 62.1 %copy-start.160 = (f32[3072]{0:T(1024)S(1)}, f32[3072]{0:T(1024)}, u32[]{:S(2)}) copy-start(f32[3072]{0:T(1024)} %get-tuple-element.309) | copy-start | bytes 36868
  230.9 62.1 %copy-start.245 = (bf16[1,128]{1,0:T(2,128)(2,1)S(1)}, bf16[1,128]{1,0:T(2,128)(2,1)}, u32[]{:S(2)}) copy-start(bf16[1,128]{1,0:T(2,128)(2,1)} %get-tuple-element.271) | copy-start | bytes 772
  230.9 129.9 %all-gather.29.cloned.1.call-start = ((), (), s32[]{:S(2)}) async-start(), calls=%async_computation.30 | async-start | bytes 1179648 | tf_op jit(solution)/shard_map/all_gather | solution.py:48
  253.8 132.2 %all-gather.19.cloned.1.call-start = ((), (), s32[]{:S(2)}) async-start(), calls=%async_computation.23 | async-start | bytes 1179648 | tf_op jit(solution)/shard_map/all_gather | solution.py:48
  288.7 105.8 %all-to-all-start = ((bf16[8,2,256,128]{3,2,1,0:T(8,128)(2,1)}), bf16[8,2,256,128]{3,2,1,0:T(8,128)(2,1)}, u32[]{:S(2)}, u32[]{:S(2)}) async-start(bf16[8,2,256,128]{3,2,1,0:T(8,128)(2,1)} %broadcast_in_dim.89), calls=%async_computation.4 | async-start | bytes 2097152 | tf_op jit(solution)/shard_map/all_to_all | solution.py:54
  292.9 146.9 %all-gather.23.cloned.1.call-start = ((), (), s32[]{:S(2)}) async-start(), calls=%async_computation.25 | async-start | bytes 2359296 | tf_op jit(solution)/shard_map/all_gather | solution.py:36
  313.6 77.1 %copy-start.241 = (f32[3,128]{1,0:T(4,128)}, f32[3,128]{1,0:T(4,128)S(1)}, u32[]{:S(2)}) copy-start(f32[3,128]{1,0:T(4,128)S(1)} %constant_dynamic-slice_fusion.3) | copy-start | bytes 4612
  314.9 75.8 %copy-start.234 = (f32[1,1024]{1,0:T(1,128)}, f32[1,1024]{1,0:T(1,128)S(1)}, u32[]{:S(2)}) copy-start(f32[1,1024]{1,0:T(1,128)S(1)} %get-tuple-element.227) | copy-start | bytes 12292
  314.9 212.8 %copy-start.165 = (f32[1,1024]{1,0:T(1,128)}, f32[1,1024]{1,0:T(1,128)S(1)}, u32[]{:S(2)}) copy-start(f32[1,1024]{1,0:T(1,128)S(1)} %get-tuple-element.226) | copy-start | bytes 12292
  395.6 19.4 %all-to-all-start.4 = ((bf16[8,2,256,128]{3,2,1,0:T(8,128)(2,1)}), bf16[8,2,256,128]{3,2,1,0:T(8,128)(2,1)S(1)}, u32[]{:S(2)}, u32[]{:S(2)}) async-start(bf16[8,2,256,128]{3,2,1,0:T(8,128)(2,1)} %broadcast_in_dim.99), calls=%async_computation.10 | async-start | bytes 2097152 | tf_op jit(solution)/shard_map/all_to_all | solution.py:54
  399.2 89.3 %all-gather.31.cloned.1.call-start = ((), (), s32[]{:S(2)}) async-start(), calls=%async_computation.31 | async-start | bytes 2359296 | tf_op jit(solution)/shard_map/all_gather | solution.py:36
  415.1 117.0 %copy-start.25 = (bf16[8,2,256,128]{3,2,1,0:T(8,128)(2,1)}, bf16[8,2,256,128]{3,2,1,0:T(8,128)(2,1)S(1)}, u32[]{:S(2)}) copy-start(bf16[8,2,256,128]{3,2,1,0:T(8,128)(2,1)S(1)} %all-to-all-done.4) | copy-start | bytes 3145732
  420.7 118.1 %reduce-scatter.23.cloned.1.call-start = ((), (), s32[]{:S(2)}) async-start(), calls=%async_computation.34 | async-start | bytes 2359296 | tf_op jit(solution)/shard_map/reduce_scatter | solution.py:75
  468.7 109.3 %reduce-scatter.27.cloned.1.call-start = ((), (), s32[]{:S(2)}) async-start(), calls=%async_computation.36 | async-start | bytes 2359296 | tf_op jit(solution)/shard_map/reduce_scatter | solution.py:75
  538.8 41.7 %copy-start.74 = (f32[2,256,2,64]{1,3,2,0:T(8,128)}, f32[2,256,2,64]{1,3,2,0:T(8,128)S(1)}, u32[]{:S(2)}) copy-start(f32[2,256,2,64]{1,3,2,0:T(8,128)S(1)} %fusion.101) | copy-start | bytes 786436
  608.7 20.7 %all-to-all-start.1 = ((bf16[8,2,256,128]{3,2,1,0:T(8,128)(2,1)}), bf16[8,2,256,128]{3,2,1,0:T(8,128)(2,1)}, u32[]{:S(2)}, u32[]{:S(2)}) async-start(bf16[8,2,256,128]{3,2,1,0:T(8,128)(2,1)} %bitcast.639), calls=%async_computation.6 | async-start | bytes 2097152 | tf_op jit(solution)/shard_map/all_to_all | solution.py:86
  629.4 19.4 %all-to-all-start.5 = ((bf16[8,2,256,128]{3,2,1,0:T(8,128)(2,1)}), bf16[8,2,256,128]{3,2,1,0:T(8,128)(2,1)S(1)}, u32[]{:S(2)}, u32[]{:S(2)}) async-start(bf16[8,2,256,128]{3,2,1,0:T(8,128)(2,1)} %bitcast.638), calls=%async_computation.12 | async-start | bytes 2097152 | tf_op jit(solution)/shard_map/all_to_all | solution.py:86
  633.0 118.8 %reduce-scatter.17.cloned.1.call-start = ((), (), s32[]{:S(2)}) async-start(), calls=%async_computation.26 | async-start | bytes 1179648 | tf_op jit(solution)/shard_map/reduce_scatter | solution.py:47
  653.1 21.6 %all-to-all-start.6 = ((bf16[8,2,256,128]{3,2,1,0:T(8,128)(2,1)}), bf16[8,2,256,128]{3,2,1,0:T(8,128)(2,1)S(1)}, u32[]{:S(2)}, u32[]{:S(2)}) async-start(bf16[8,2,256,128]{3,2,1,0:T(8,128)(2,1)} %broadcast_in_dim.104), calls=%async_computation.13 | async-start | bytes 2097152 | tf_op jit(solution)/shard_map/all_to_all | solution.py:54
  656.7 103.4 %reduce-scatter.21.cloned.1.call-start = ((), (), s32[]{:S(2)}) async-start(), calls=%async_computation.32 | async-start | bytes 1179648 | tf_op jit(solution)/shard_map/reduce_scatter | solution.py:47
  665.5 144.7 %reduce-scatter.29.cloned.1.call-start = ((), (), s32[]{:S(2)}) async-start(), calls=%async_computation.37 | async-start | bytes 2359296 | tf_op jit(solution)/shard_map/reduce_scatter | solution.py:75
  704.6 19.4 %all-to-all-start.2 = ((bf16[8,2,256,128]{3,2,1,0:T(8,128)(2,1)}), bf16[8,2,256,128]{3,2,1,0:T(8,128)(2,1)S(1)}, u32[]{:S(2)}, u32[]{:S(2)}) async-start(bf16[8,2,256,128]{3,2,1,0:T(8,128)(2,1)} %broadcast_in_dim.94), calls=%async_computation.7 | async-start | bytes 2097152 | tf_op jit(solution)/shard_map/all_to_all | solution.py:54
  708.1 117.9 %reduce-scatter.25.cloned.1.call-start = ((), (), s32[]{:S(2)}) async-start(), calls=%async_computation.35 | async-start | bytes 2359296 | tf_op jit(solution)/shard_map/reduce_scatter | solution.py:75
  751.7 208.2 %all-gather.25.cloned.1.call-start = ((), (), s32[]{:S(2)}) async-start(), calls=%async_computation.27 | async-start | bytes 1179648 | tf_op jit(solution)/shard_map/all_gather | solution.py:48
  752.3 207.6 %all-gather.33.cloned.1.call-start = ((), (), s32[]{:S(2)}) async-start(), calls=%async_computation.33 | async-start | bytes 1179648 | tf_op jit(solution)/shard_map/all_gather | solution.py:48
  760.1 220.6 %reduce-scatter.33.cloned.1.call-start = ((), (), s32[]{:S(2)}) async-start(), calls=%async_computation.39 | async-start | bytes 3342336
  781.0 223.4 %reduce-scatter.31.cloned.1.call-start = ((), (), s32[]{:S(2)}) async-start(), calls=%async_computation.38 | async-start | bytes 3342336
  859.0 81.9 %copy-start.225 = (f32[2,256]{1,0:T(2,128)S(1)}, f32[2,256]{1,0:T(2,128)}, u32[]{:S(2)}) copy-start(f32[2,256]{1,0:T(2,128)} %get-tuple-element.122) | copy-start | bytes 6148
  937.6 8.7 all-to-all-start.9
  946.9 8.7 all-to-all-start.8
  955.6 20.2 %all-to-all-start.7 = ((bf16[8,2,256,128]{3,2,1,0:T(8,128)(2,1)}), bf16[8,2,256,128]{3,2,1,0:T(8,128)(2,1)}, u32[]{:S(2)}, u32[]{:S(2)}) async-start(bf16[8,2,256,128]{3,2,1,0:T(8,128)(2,1)} %bitcast_bitcast_fusion), calls=%async_computation.15 | async-start | bytes 2097152 | tf_op jit(solution)/shard_map/all_to_all | solution.py:86
  975.8 19.5 %all-to-all-start.3 = ((bf16[8,2,256,128]{3,2,1,0:T(8,128)(2,1)}), bf16[8,2,256,128]{3,2,1,0:T(8,128)(2,1)S(1)}, u32[]{:S(2)}, u32[]{:S(2)}) async-start(bf16[8,2,256,128]{3,2,1,0:T(8,128)(2,1)} %bitcast.611), calls=%async_computation.9 | async-start | bytes 2097152 | tf_op jit(solution)/shard_map/all_to_all | solution.py:86
  (240 other events, 1101.1 us)
Sparse Core Ops, SparseCore 0:
  12.6 50.5 all-gather.14
  122.7 46.9 all-gather.26
  171.9 46.4 all-gather.16
  220.6 33.1 reduce-scatter.18
  256.6 30.7 reduce-scatter.14
  290.0 46.4 all-gather.20
  338.3 22.5 all-gather.28
  362.5 23.4 all-gather.18
  394.6 45.2 all-gather.22
  441.8 46.5 all-gather.30
  490.9 43.5 reduce-scatter.22
  536.7 41.2 reduce-scatter.26
  641.5 36.3 reduce-scatter.16
  680.1 30.1 reduce-scatter.20
  713.2 41.1 reduce-scatter.28
  756.7 41.6 reduce-scatter.24
  800.0 22.3 all-gather.24
  823.9 23.4 all-gather.32
  850.7 75.4 reduce-scatter.32
  929.5 74.8 reduce-scatter.30
where the time goes:
time: 1030 us; the launch traced here: 1020 us
  waiting for transfers between devices  347 us (34%)
  blocking collectives  185 us (18%)
  matrix products  163 us (16%)
  other arithmetic  134 us (13%)
  local copies, waits for them, and re-layouts  129 us (13%)
  starting transfers between devices  40.2 us (4%)
  between operations  20.5 us (2%)
    unnamed x2, blocking collectives  147 us
    all_gather x4, waiting for transfers between devices, side_by_side_2(): lax.all_gather(both, axis, axis=dim, tiled=True)  95 us
    reduce_scatter x4, waiting for transfers between devices, total_of(): own = lax.psum_scatter(padded, axis, scatter_dimension=0, tiled=True)  56.4 us
    all_gather x4, waiting for transfers between devices, total_of(): whole = lax.all_gather(own, axis, axis=0, tiled=True)  47.2 us
    all_to_all x6, waiting for transfers between devices, sent_to_all(): return lax.all_to_all(copies, axis, split_axis=0, concat_axis=0, tiled=True)  42.9 us
    unnamed x546, local copies, waits for them, and re-layouts  39.6 us
    all_to_all x4, waiting for transfers between devices, sent_and_summed(): tiles = lax.all_to_all(in_blocks(shard, dim, size), axis, 0, 0, tiled=True)  39.5 us
    all_gather x2, blocking collectives, gather_layer(): lax.all_gather(norm_gain[layer_id], ('dp', 'seq'), axis=0, tiled=True)  37.6 us
  transfers between devices with their start and end apart: 30, of which 20 were waited for; matrix products, arithmetic and copies ran while one was open for 34% of the time, Pallas kernels for 0%

commit v1 on v0

v1 whole, which is shorter than its diff:
```python
import math

import jax
import jax.numpy as jnp
from jax import lax
from jax.experimental import pallas as pl
from jax.experimental.pallas import tpu as pltpu
from jax.sharding import PartitionSpec as P

D = 1024
FF = 4096
HEAD = 64
ROT = 16
LAYERS = 2
DOCUMENTS = 5
BLOCK = 256
VMEM_BYTES = 48 * 1024 * 1024
OWNERS = ("dp", "seq")
PLACES = ("seq", "tensor")
ALONG_Z = [[2 * z + core for z in range(4)] for core in range(2)]
ALONG_CORE = [[2 * z + core for core in range(2)] for z in range(4)]

epsilon = 1e-05


def dot(a, b, dims):
    return lax.dot_general(a, b, (dims, ((), ())), preferred_element_type=jnp.float32)


def turned(block, cosine, sines):
    half = ROT // 2
    low, high = (block[:half], block[half:ROT])
    return jnp.concatenate(
        [low * cosine - high * sines, high * cosine + low * sines, block[ROT:]], axis=0
    )


def prepare(packed, table, keys, keys_t, values, blocks):
    queries = []
    half = ROT // 2
    for i in range(blocks):
        cols = slice(i * BLOCK, (i + 1) * BLOCK)
        cosine, sines = (table[:half, cols], table[half:, cols])
        query = turned(packed[i, 0].astype(jnp.float32), cosine, sines).astype(jnp.bfloat16)
        queries.append(query * jnp.bfloat16(HEAD**-0.5))
        key = turned(packed[i, 1].astype(jnp.float32), cosine, sines).astype(jnp.bfloat16)
        keys[cols, :] = key.T
        if keys_t is not None:
            keys_t[:, cols] = key
        if values is not None:
            values[cols, :] = packed[i, 2].T
    return queries


def permitted(i, starts):
    length = (i + 1) * BLOCK
    row = lax.broadcasted_iota(jnp.int32, (length, BLOCK), 0)
    col = lax.broadcasted_iota(jnp.int32, (length, BLOCK), 1) + i * BLOCK
    return (row >= starts) & (row <= col)


def attend_kernel(packed, table, starts, out, wide, log_total, keys, values_t):
    blocks = packed.shape[0]
    queries = prepare(packed, table, keys, None, None, blocks)
    for i in range(blocks):
        values_t[:, i * BLOCK : (i + 1) * BLOCK] = packed[i, 2]
    for i in range(blocks):
        length = (i + 1) * BLOCK
        scores = dot(keys[:length], queries[i], ((1,), (0,)))
        allowed = permitted(i, starts[:, i * BLOCK : length])
        scores = jnp.where(allowed, scores, -1e30)
        largest = jnp.max(scores, axis=0, keepdims=True)
        exponent = jnp.exp(scores - largest)
        total = jnp.sum(exponent, axis=0, keepdims=True)
        result = dot(values_t[:, :length], exponent.astype(jnp.bfloat16), ((1,), (0,)))
        result = result / total
        wide[i] = result
        out[i] = result.astype(jnp.bfloat16)
        log_total[i] = largest + jnp.log(total)


def attend(packed, table, starts):
    blocks = packed.shape[0]
    full = blocks * BLOCK
    return pl.pallas_call(
        attend_kernel,
        out_shape=(
            jax.ShapeDtypeStruct((blocks, HEAD, BLOCK), jnp.bfloat16),
            jax.ShapeDtypeStruct((blocks, HEAD, BLOCK), jnp.float32),
            jax.ShapeDtypeStruct((blocks, 1, BLOCK), jnp.float32),
        ),
        scratch_shapes=[
            pltpu.VMEM((full, HEAD), jnp.bfloat16),
            pltpu.VMEM((HEAD, full), jnp.bfloat16),
        ],
        compiler_params=pltpu.CompilerParams(vmem_limit_bytes=VMEM_BYTES),
        cost_estimate=pl.CostEstimate(
            flops=4 * full * full * HEAD, bytes_accessed=2**21, transcendentals=full * full // 2
        ),
    )(packed, table, starts)


def attend_back_kernel(
    packed, table, starts, wide, log_total, upper, out, keys, keys_t, values, grad_k, grad_v
):
    blocks = packed.shape[0]
    half = ROT // 2
    queries = prepare(packed, table, keys, keys_t, values, blocks)
    for i in range(blocks):
        length = (i + 1) * BLOCK
        cols = slice(i * BLOCK, length)
        scores = dot(keys[:length], queries[i], ((1,), (0,)))
        allowed = permitted(i, starts[:, cols])
        probs = jnp.exp(jnp.where(allowed, scores, -1e30) - log_total[i])
        above = upper[i]
        grad_probs = dot(values[:length], above, ((1,), (0,)))
        row_dot = jnp.sum(above.astype(jnp.float32) * wide[i], axis=0, keepdims=True)
        grad_scores = (probs * (grad_probs - row_dot)).astype(jnp.bfloat16)
        grad_q = dot(keys_t[:, :length], grad_scores, ((1,), (0,))) * HEAD**-0.5
        cosine, sines = (table[:half, cols], table[half:, cols])
        out[i, 0] = turned(grad_q, cosine, -sines).astype(jnp.bfloat16)
        probs_low = probs.astype(jnp.bfloat16)
        part_v = dot(above, probs_low, ((1,), (1,)))
        part_k = dot(queries[i], grad_scores, ((1,), (1,)))
        if i > 0:
            grad_v[:, : i * BLOCK] += part_v[:, : i * BLOCK]
            grad_k[:, : i * BLOCK] += part_k[:, : i * BLOCK]
        grad_v[:, cols] = part_v[:, cols]
        grad_k[:, cols] = part_k[:, cols]
    for i in range(blocks):
        cols = slice(i * BLOCK, (i + 1) * BLOCK)
        cosine, sines = (table[:half, cols], table[half:, cols])
        out[i, 1] = turned(grad_k[:, cols], cosine, -sines).astype(jnp.bfloat16)
        out[i, 2] = grad_v[:, cols].astype(jnp.bfloat16)


def attend_back(packed, table, starts, wide, log_total, upper):
    blocks = packed.shape[0]
    full = blocks * BLOCK
    return pl.pallas_call(
        attend_back_kernel,
        out_shape=jax.ShapeDtypeStruct((blocks, 3, HEAD, BLOCK), jnp.bfloat16),
        scratch_shapes=[
            pltpu.VMEM((full, HEAD), jnp.bfloat16),
            pltpu.VMEM((HEAD, full), jnp.bfloat16),
            pltpu.VMEM((full, HEAD), jnp.bfloat16),
            pltpu.VMEM((HEAD, full), jnp.float32),
            pltpu.VMEM((HEAD, full), jnp.float32),
        ],
        compiler_params=pltpu.CompilerParams(vmem_limit_bytes=VMEM_BYTES),
        cost_estimate=pl.CostEstimate(
            flops=10 * full * full * HEAD, bytes_accessed=2**22, transcendentals=full * full // 2
        ),
    )(packed, table, starts, wide, log_total, upper)


def exchange(blocks, axis, groups=None):
    return lax.all_to_all(blocks, axis, 0, 0, tiled=True, axis_index_groups=groups)


def sent_to_all(shard, axis, groups=None):
    size = lax.axis_size(axis) if groups is None else len(groups[0])
    return exchange(jnp.broadcast_to(shard, (size, *shard.shape)), axis, groups)


def gathered(shard):
    return sent_to_all(sent_to_all(shard, "tensor", ALONG_Z), "tensor", ALONG_CORE)


def summed_share(blocks):
    halves = exchange(blocks.astype(jnp.bfloat16), "tensor", ALONG_CORE).astype(jnp.float32)
    half = (halves[0] + halves[1]).astype(jnp.bfloat16)
    return jnp.sum(exchange(half, "tensor", ALONG_Z).astype(jnp.float32), axis=0)


def gathered_tokens(own):
    every = gathered(own).reshape(2, 4, 4, 32, own.shape[-1])
    return every.transpose(2, 1, 0, 3, 4).reshape(-1, own.shape[-1])


def summed_tokens(partial):
    width = partial.shape[-1]
    blocks = partial.reshape(4, 4, 2, 32, width).transpose(2, 1, 0, 3, 4)
    return summed_share(blocks).reshape(-1, width)


def own_rows(tokens, rank):
    width = tokens.shape[-1]
    rows = lax.dynamic_index_in_dim(tokens.reshape(4, 8, 32, width), rank, 1, False)
    return rows.reshape(-1, width)


def normalised(values):
    centred = values - jnp.mean(values, axis=-1, keepdims=True)
    variance = jnp.mean(centred * centred, axis=-1, keepdims=True)
    scale = lax.rsqrt(variance + epsilon)
    return centred * scale, scale


def norm_back(grad, hat, scale):
    mean = jnp.mean(grad, axis=-1, keepdims=True)
    along = jnp.mean(grad * hat, axis=-1, keepdims=True)
    return scale * (grad - mean - hat * along)


def gelu_and_slope(values):
    share = 0.5 * (1.0 + lax.erf(values * math.sqrt(0.5)))
    slope = share + values * jnp.exp(-0.5 * values * values) * (1.0 / math.sqrt(2.0 * math.pi))
    return (values * share).astype(jnp.bfloat16), slope


def low(values):
    return values.astype(jnp.bfloat16)


def shards(inputs, w_qkv, w_dense, w_fc1, w_fc2, norm_gain, biases, segment_ids, cotangent):
    tensor_rank = lax.axis_index("tensor")
    seq_rank = lax.axis_index("seq")
    owners = 16
    full_len = segment_ids.shape[1]
    head_cols = w_qkv.shape[3]
    hidden_cols = w_fc1.shape[2]
    share = w_qkv.shape[1]
    gain_share = norm_gain.shape[1]
    bias_share = biases.shape[1]
    mine = jnp.arange(8) == tensor_rank

    qkv_flat = w_qkv.reshape(LAYERS, share, 3 * head_cols)
    vectors = jnp.concatenate([norm_gain, biases], axis=1).reshape(-1)
    rows = 16
    vectors = jnp.pad(vectors, (0, rows * 3 * head_cols - vectors.size)).reshape(rows, -1)
    first = sent_to_all(jnp.concatenate([qkv_flat[0], vectors], axis=0), OWNERS)
    qkv_zero = first[:, :share].reshape(D, 3 * head_cols)
    vectors = first[:, share:].reshape(owners, -1)[:, : LAYERS * (gain_share + bias_share)]
    vectors = vectors.reshape(owners, LAYERS, -1).astype(jnp.float32)
    gain_vecs = [vectors[:, l, :gain_share].reshape(-1) for l in range(LAYERS)]
    bias_vecs = [vectors[:, l, gain_share:].reshape(-1) for l in range(LAYERS)]

    both_fc = lax.all_gather(
        jnp.concatenate([w_fc1[0], w_fc2[0]], axis=1), OWNERS, axis=0, tiled=True
    )
    dense_whole = lax.all_gather(w_dense[0], (*OWNERS, "tensor"), axis=0, tiled=True)
    dense_whole = dense_whole.reshape(owners, 8, share, head_cols).transpose(0, 2, 1, 3)
    dense_whole = dense_whole.reshape(D, D)
    later = lax.all_gather(
        jnp.concatenate([qkv_flat[1], w_dense[1], w_fc1[1], w_fc2[1]], axis=1),
        OWNERS,
        axis=0,
        tiled=True,
    )
    ends = [3 * head_cols, 4 * head_cols, 4 * head_cols + hidden_cols]
    qkv_one, dense_one, fc1_one, fc2_one = jnp.split(later, ends, axis=1)
    qkv_weights = [qkv_zero, qkv_one]
    fc1_weights = [both_fc[:, :hidden_cols], fc1_one]
    fc2_weights = [both_fc[:, hidden_cols:], fc2_one]

    gains, shifts, qkv_biases, fc1_biases, outer_biases = ([], [], [], [], [])
    for l in range(LAYERS):
        vec = bias_vecs[l]
        gains.append((gain_vecs[l][:D], gain_vecs[l][D:]))
        shifts.append((vec[:D], vec[D : 2 * D]))
        qkv_biases.append(
            lax.dynamic_index_in_dim(vec[2 * D : 5 * D].reshape(3, 8, -1), tensor_rank, 1, False)
        )
        fc1_biases.append(
            lax.dynamic_index_in_dim(vec[6 * D : 6 * D + FF].reshape(8, -1), tensor_rank, 0, False)
        )
        outer_biases.append(vec[5 * D : 6 * D] + vec[6 * D + FF :])

    segments = lax.dynamic_index_in_dim(segment_ids, seq_rank // 2, 0, False)
    earlier = jnp.zeros_like(segments)
    for doc in range(1, DOCUMENTS):
        before = jnp.sum((segments < doc).astype(jnp.int32))
        earlier = jnp.where(segments == doc, before, earlier)
    places = jnp.arange(full_len, dtype=jnp.int32) - earlier
    half_rot = ROT // 2
    inverse = 10000.0 ** (-jnp.arange(half_rot, dtype=jnp.float32) * 2.0 / ROT)
    angles = inverse[:, None] * places.astype(jnp.float32)[None, :]
    table = jnp.concatenate([jnp.cos(angles), jnp.sin(angles)], axis=0)
    starts = earlier[None, :]

    def project(normed, l):
        weight = qkv_weights[l]
        flat = dot(weight, normed, ((0,), (1,)))
        flat = low(flat + qkv_biases[l].reshape(-1)[:, None])
        blocks = flat.reshape(3, 2, HEAD, 4, BLOCK).transpose(3, 1, 0, 2, 4)
        return exchange(blocks.reshape(8, 3, HEAD, BLOCK), "seq")

    def to_columns(blocks):
        back = exchange(blocks, "seq").reshape(4, 2, HEAD, BLOCK)
        return back.transpose(1, 2, 0, 3).reshape(2 * HEAD, 4 * BLOCK)

    start = inputs.reshape(-1, D)
    hat_zero, scale_zero = normalised(start.astype(jnp.float32))
    normed = [[low(hat_zero * gains[0][k] + shifts[0][k]) for k in range(2)]]
    attention, attended, hidden, slopes = ([], [], [], [])

    def hidden_of(l):
        pre_act = dot(normed[l][1], fc1_weights[l], ((1,), (0,))) + fc1_biases[l]
        activated, slope = gelu_and_slope(pre_act)
        hidden.append(activated)
        slopes.append(slope)

    packed = project(normed[0][0], 0)
    hidden_of(0)
    branch = summed_tokens(dot(hidden[0], fc2_weights[0], ((1,), (1,))))
    result, wide, log_total = attend(packed, table, starts)
    attention.append((packed, wide, log_total))
    sent = result.reshape(8, HEAD, 8, 32).transpose(0, 2, 3, 1).reshape(64, 16, 2 * HEAD)
    heads = exchange(sent, PLACES).reshape(4, 2, 8, 32, HEAD)
    heads = heads.transpose(0, 3, 2, 1, 4).reshape(-1, D)
    attended.append(to_columns(result))
    residual = own_rows(start, tensor_rank).astype(jnp.float32)
    residual = residual + (dot(heads, dense_whole, ((1,), (1,))) + branch + outer_biases[0])

    hat_one, scale_one = normalised(residual)
    hat_low = gathered_tokens(low(hat_one)).astype(jnp.float32)
    normed.append([low(hat_low * gains[1][k] + shifts[1][k]) for k in range(2)])
    packed = project(normed[1][0], 1)
    hidden_of(1)
    result, wide, log_total = attend(packed, table, starts)
    attention.append((packed, wide, log_total))
    attended.append(to_columns(result))
    partial = dot(attended[1], dense_one, ((0,), (1,)))
    partial = partial + dot(hidden[1], fc2_weights[1], ((1,), (1,)))
    final = residual + (summed_tokens(partial) + outer_biases[1])
    block_out = gathered_tokens(low(final)).reshape(inputs.shape)

    grad_low = gathered(cotangent.reshape(-1, cotangent.shape[-1]))
    grad_low = grad_low.transpose(2, 1, 0, 3).reshape(-1, D)
    grad_own = own_rows(grad_low, tensor_rank).astype(jnp.float32)
    flat_grads, small = ([None] * LAYERS, [None] * LAYERS)
    for l in reversed(range(LAYERS)):
        grad_own_low = low(grad_own)
        if l < LAYERS - 1:
            grad_low = gathered_tokens(grad_own_low)
            upper = low(dot(grad_own_low, dense_whole, ((1,), (0,))))
            upper = upper.reshape(4, 32, 8, 2, HEAD).transpose(0, 3, 2, 1, 4)
            upper = exchange(upper.reshape(64, 16, 2 * HEAD), PLACES)
            upper = upper.reshape(8, 8, 32, HEAD).transpose(0, 3, 1, 2)
            upper = upper.reshape(8, HEAD, BLOCK)
        else:
            upper = low(dot(dense_one, grad_low, ((0,), (1,))))
            upper = upper.reshape(2, HEAD, 4, BLOCK).transpose(2, 0, 1, 3)
            upper = exchange(upper.reshape(8, HEAD, BLOCK), "seq")
        grad_dense = dot(grad_low, attended[l], ((0,), (1,)))
        grad_fc2 = dot(grad_low, hidden[l], ((0,), (0,)))
        grad_pre = low(dot(grad_low, fc2_weights[l], ((1,), (0,))) * slopes[l])
        grad_fc1 = dot(normed[l][1], grad_pre, ((0,), (0,)))
        grad_two = dot(grad_pre, fc1_weights[l], ((1,), (1,)))
        packed, wide, log_total = attention[l]
        grad_heads = exchange(attend_back(packed, table, starts, wide, log_total, upper), "seq")
        grad_heads = grad_heads.reshape(4, 2, 3, HEAD, BLOCK).transpose(2, 1, 3, 0, 4)
        grad_heads = grad_heads.reshape(3 * head_cols, 4 * BLOCK)
        grad_qkv = dot(normed[l][0], grad_heads, ((0,), (1,)))
        grad_one = dot(grad_heads, qkv_weights[l], ((0,), (1,)))
        combined = grad_one * gains[l][0] + grad_two * gains[l][1]
        if l > 0:
            grad_own = grad_own + norm_back(summed_tokens(combined), hat_one, scale_one)
        else:
            change = norm_back(combined, hat_zero, scale_zero)
            blocks = change.reshape(-1, 4, 2, D // 8).transpose(2, 1, 0, 3)
            columns = lax.dynamic_slice_in_dim(grad_low, tensor_rank * (D // 8), D // 8, 1)
            grad_inputs = columns.astype(jnp.float32) + summed_share(blocks)
            grad_inputs = grad_inputs.reshape(cotangent.shape)
        if l > 0:
            both = jnp.concatenate(
                [low(grad_qkv), low(grad_dense), low(grad_fc1), low(grad_fc2)], axis=1
            )
            both = lax.psum_scatter(both, OWNERS, scatter_dimension=0, tiled=True)
            flat_grads[l] = jnp.split(both.astype(jnp.float32), ends, axis=1)
        else:
            both = jnp.concatenate([low(grad_dense), low(grad_fc1), low(grad_fc2)], axis=1)
            both = lax.psum_scatter(both, OWNERS, scatter_dimension=0, tiled=True)
            others = jnp.split(
                both.astype(jnp.float32), [head_cols, head_cols + hidden_cols], axis=1
            )
            tiles = exchange(low(grad_qkv).reshape(owners, share, -1), OWNERS)
            flat_grads[l] = [jnp.sum(tiles.astype(jnp.float32), axis=0), *others]
        head_sums = jnp.sum(grad_heads.astype(jnp.float32), axis=1)
        pre_sums = jnp.sum(grad_pre.astype(jnp.float32), axis=0)
        own_sums = jnp.sum(grad_own_low.astype(jnp.float32), axis=0)
        shift_grads, gain_grads = ([], [])
        for k, (weight, grad_weight, sums) in enumerate(
            ((qkv_weights[l], grad_qkv, head_sums), (fc1_weights[l], grad_fc1, pre_sums))
        ):
            wide_weight = weight.astype(jnp.float32)
            shift_grad = jnp.sum(wide_weight * sums, axis=1)
            product = jnp.sum(wide_weight * grad_weight, axis=1)
            shift_grads.append(shift_grad)
            gain_grads.append((product - shifts[l][k] * shift_grad) / gains[l][k])
        placed_heads = jnp.where(mine[:, None], head_sums.reshape(3, 1, head_cols), 0.0)
        placed_pre = jnp.where(mine[:, None], pre_sums[None, :], 0.0)
        bias_grad = jnp.concatenate(
            [*shift_grads, placed_heads.reshape(-1), own_sums, placed_pre.reshape(-1), own_sums]
        )
        small[l] = jnp.concatenate(
            [
                bias_grad.reshape(owners, bias_share),
                jnp.concatenate(gain_grads).reshape(owners, gain_share),
            ],
            axis=1,
        )
    small = jnp.sum(exchange(jnp.concatenate(small, axis=1), OWNERS), axis=0)
    small = jnp.sum(sent_to_all(small, "tensor"), axis=0).reshape(LAYERS, -1)
    stacked = [jnp.stack([flat_grads[l][k] for l in range(LAYERS)]) for k in range(4)]
    return (
        block_out,
        grad_inputs,
        stacked[0].reshape(w_qkv.shape),
        stacked[1],
        stacked[2],
        stacked[3],
        small[:, bias_share:],
        small[:, :bias_share],
    )


def solution(mesh):
    in_specs = (
        P("dp", "seq", None),
        P(None, ("dp", "seq"), None, "tensor"),
        P(None, ("dp", "seq"), "tensor"),
        P(None, ("dp", "seq"), "tensor"),
        P(None, ("dp", "seq"), "tensor"),
        P(None, ("dp", "seq")),
        P(None, ("dp", "seq")),
        P("dp", None),
        P("dp", "seq", "tensor"),
    )
    out_specs = (
        P("dp", "seq", None),
        P("dp", "seq", "tensor"),
        P(None, ("dp", "seq"), None, "tensor"),
        P(None, ("dp", "seq"), "tensor"),
        P(None, ("dp", "seq"), "tensor"),
        P(None, ("dp", "seq"), "tensor"),
        P(None, ("dp", "seq")),
        P(None, ("dp", "seq")),
    )
    return jax.shard_map(shards, mesh=mesh, in_specs=in_specs, out_specs=out_specs, check_vma=False)
```

time: 1030 us -> 587 us (0.57)
  waiting for transfers between devices: 347 us -> 150 us
  blocking collectives: 185 us -> 46.2 us
  matrix products: 163 us -> 65.5 us
  other arithmetic: 134 us -> 52.1 us
  starting transfers between devices: 40.2 us -> 104 us
  Pallas kernels: 0 us -> 28.8 us
  local copies, waits for them, and re-layouts: 129 us -> 116 us
    unnamed x2 -> x0, blocking collectives: 147 us -> none
    all_gather x10 -> x3, waiting for transfers between devices: 164 us -> 18.6 us  [the longest x1 18.6 us: shards(): lax.all_gather(w_dense[0], (*OWNERS, 'tensor'), axis=0, tiled=True)]
    dot_general x72 -> x24, matrix products: 163 us -> 65.5 us  [dot(): lax.dot_general(a, b, (dims, ((), ())), preferred_element_type=jnp.float32)]
    reduce_scatter x8 -> x0, waiting for transfers between devices: 92.3 us -> none  [the longest x4 56.4 us: total_of(): own = lax.psum_scatter(padded, axis, scatter_dimension=0, tiled=True)]
    all_to_all x10 -> x22, starting transfers between devices: 37.6 us -> 103 us  [exchange(): lax.all_to_all(blocks, axis, 0, 0, tiled=True, axis_index_groups=groups)]
    all_to_all x10 -> x22, waiting for transfers between devices: 82.4 us -> 131 us  [exchange(): lax.all_to_all(blocks, axis, 0, 0, tiled=True, axis_index_groups=groups)]
    all_to_all x0 -> x7, blocking collectives: none -> 46.2 us  [exchange(): lax.all_to_all(blocks, axis, 0, 0, tiled=True, axis_index_groups=groups)]
    all_gather x2 -> x0, blocking collectives: 37.6 us -> none  [gather_layer(): lax.all_gather(norm_gain[layer_id], ('dp', 'seq'), axis=0, tiled=True)]
  transfers between devices with their start and end apart: 30 -> 27, of which waited for: 20 -> 18; matrix products, arithmetic and copies ran while one was open for 34% -> 34% of each run, Pallas kernels for 0% -> 5%
where the time goes in v1:
time: 587 us; the launch traced here: 578 us
  waiting for transfers between devices  150 us (26%)
  local copies, waits for them, and re-layouts  116 us (20%)
  starting transfers between devices  104 us (18%)
  matrix products  65.5 us (11%)
  other arithmetic  52.1 us (9%)
  blocking collectives  46.2 us (8%)
  Pallas kernels  28.8 us (5%)
  between operations  15.6 us (3%)
    all_to_all x22, waiting for transfers between devices, exchange(): lax.all_to_all(blocks, axis, 0, 0, tiled=True, axis_index_groups=groups)  131 us
    all_to_all x22, starting transfers between devices, exchange(): lax.all_to_all(blocks, axis, 0, 0, tiled=True, axis_index_groups=groups)  103 us
    dot_general x24, matrix products, dot(): lax.dot_general(a, b, (dims, ((), ())), preferred_element_type=jnp.float32)  65.5 us
    all_to_all x7, blocking collectives, exchange(): lax.all_to_all(blocks, axis, 0, 0, tiled=True, axis_index_groups=groups)  46.2 us
    unnamed x205, local copies, waits for them, and re-layouts  36.8 us
    all_gather x1, waiting for transfers between devices, shards(): lax.all_gather(w_dense[0], (*OWNERS, 'tensor'), axis=0, tiled=True)  18.6 us
    pallas_call x2, Pallas kernels, attend_back(): pl.pallas_call(attend_back_kernel, out_shape=jax.ShapeDtypeStruct((blocks...  14.9 us
    pallas_call x2, Pallas kernels, attend(): pl.pallas_call(attend_kernel, out_shape=(jax.ShapeDtypeStruct((blocks, HE...  13.9 us
  transfers between devices with their start and end apart: 27, of which 18 were waited for; matrix products, arithmetic and copies ran while one was open for 34% of the time, Pallas kernels for 5%

profile of v1, /device:TPU:0, one launch (start us, length us, event | category | flops | bytes accessed | tf_op | source)
XLA Modules:
  0.0 577.6 jit_solution(4918655980988361407)
XLA Ops:
  13.2 7.1 %all-to-all-start = ((bf16[16,80,384]{2,1,0:T(8,128)(2,1)}), bf16[16,80,384]{2,1,0:T(8,128)(2,1)S(1)}, u32[]{:S(2)}, u32[]{:S(2)}) async-start(bf16[16,80,384]{2,1,0:T(8,128)(2,1)} %broadcast_in_dim.145), calls=%async_computation | async-start | bytes 1966080 | tf_op jit(solution)/shard_map/all_to_all | solution.py:158
  31.4 7.4 %all-to-all-done = bf16[16,80,384]{2,1,0:T(8,128)(2,1)S(1)} async-done(((bf16[16,80,384]{2,1,0:T(8,128)(2,1)}), bf16[16,80,384]{2,1,0:T(8,128)(2,1)S(1)}, u32[]{:S(2)}, u32[]{:S(2)}) %all-to-all-start) | async-done | bytes 983072 | tf_op jit(solution)/shard_map/all_to_all | solution.py:158
  53.9 4.2 add_convert_fusion.2
  58.1 10.4 %all-to-all-done.1.packed = bf16[8,3,64,256]{3,2,1,0:T(8,128)(2,1)S(1)} async-done(((bf16[8,3,64,256]{3,2,1,0:T(8,128)(2,1)}), bf16[8,3,64,256]{3,2,1,0:T(8,128)(2,1)S(1)}, u32[]{:S(2)}, u32[]{:S(2)}) %all-to-all-start.1) | async-done | bytes 786464 | tf_op jit(solution)/shard_map/all_to_all | solution.py:158
  68.5 7.0 %shard_map.152 = (bf16[8,64,256]{2,1,0:T(8,128)(2,1)}, f32[8,64,256]{2,1,0:T(8,128)S(1)}, f32[8,1,256]{2,1,0:T(1,128)S(1)}) custom-call(bf16[8,3,64,256]{3,2,1,0:T(8,128)(2,1)S(1)} %all-to-all-done.1.packed, f32[16,2048]{1,0:T(8,128)S(1)} %pad_maximum_fusion.6.table, s32[1,2048]{1,0:T(1,128)S(1)} %get-tuple-element.95.starts), custom_call_target="tpu_custom_call" | custom-call | flops 1073741824 | bytes 2097152 | tf_op jit(solution)/shard_map/pallas_call | solution.py:85
  79.4 4.8 multiply_convert_fusion.2
  85.8 6.3 %all_to_all.150 = bf16[2,4,4,32,1024]{4,3,1,2,0:T(8,128)(2,1)} all-to-all(bf16[2,4,4,32,1024]{4,3,1,2,0:T(8,128)(2,1)S(1)} %bitcast.301), channel_id=1, replica_groups={{0,1},{2,3},{4,5},{6,7},{8,9},{10,11},{12,13},{14,15},{16,17},{18,19},{..., dimensions={0} | all-to-all | bytes 4194304 | tf_op jit(solution)/shard_map/all_to_all | solution.py:158
  92.1 8.1 %all-to-all-start.2 = ((bf16[64,16,128]{2,1,0:T(8,128)(2,1)}), bf16[64,16,128]{2,1,0:T(8,128)(2,1)}, u32[]{:S(2)}, u32[]{:S(2)}) async-start(bf16[64,16,128]{2,1,0:T(8,128)(2,1)} %reshape.441), calls=%async_computation.2 | async-start | bytes 524288 | tf_op jit(solution)/shard_map/all_to_all | solution.py:158
  103.7 6.2 %all-to-all-done.2 = bf16[64,16,128]{2,1,0:T(8,128)(2,1)} async-done(((bf16[64,16,128]{2,1,0:T(8,128)(2,1)}), bf16[64,16,128]{2,1,0:T(8,128)(2,1)}, u32[]{:S(2)}, u32[]{:S(2)}) %all-to-all-start.2) | async-done | bytes 262176 | tf_op jit(solution)/shard_map/all_to_all | solution.py:158
  109.8 4.5 all-to-all-start.4
  119.6 18.6 %all-gather.9.cloned.1.call-done = bf16[1,8192,128]{2,1,0:T(8,128)(2,1)} async-done(((bf16[1,64,128]{2,1,0:T(8,128)(2,1)}), bf16[1,8192,128]{2,1,0:T(8,128)(2,1)}) %all-gather.9.cloned.1.call-update) | async-done | bytes 2097168 | tf_op jit(solution)/shard_map/all_gather | solution.py:242
  143.9 4.2 all-to-all-start.13
  152.6 11.4 %all-to-all-done.13 = bf16[4,1024,128]{1,2,0:T(8,128)(2,1)} async-done(((bf16[4,1024,128]{1,2,0:T(8,128)(2,1)}), bf16[4,1024,128]{1,2,0:T(8,128)(2,1)}, u32[]{:S(2)}, u32[]{:S(2)}) %all-to-all-start.13) | async-done | bytes 1048608 | tf_op jit(solution)/shard_map/all_to_all | solution.py:158
  170.0 13.6 %all-to-all-done.5 = bf16[4,128,1024]{2,1,0:T(8,128)(2,1)S(1)} async-done(((bf16[4,128,1024]{2,1,0:T(8,128)(2,1)}), bf16[4,128,1024]{2,1,0:T(8,128)(2,1)S(1)}, u32[]{:S(2)}, u32[]{:S(2)}) %all-to-all-start.5) | async-done | bytes 1048608 | tf_op jit(solution)/shard_map/all_to_all | solution.py:158
  183.9 5.4 all_to_all.151
  192.8 4.8 all-to-all-start.14
  217.2 6.5 %all-to-all-done.7.packed = bf16[8,3,64,256]{3,2,1,0:T(8,128)(2,1)S(1)} async-done(((bf16[8,3,64,256]{3,2,1,0:T(8,128)(2,1)}), bf16[8,3,64,256]{3,2,1,0:T(8,128)(2,1)S(1)}, u32[]{:S(2)}, u32[]{:S(2)}) %all-to-all-start.7) | async-done | bytes 786464 | tf_op jit(solution)/shard_map/all_to_all | solution.py:158
  227.9 5.0 multiply_convert_fusion.1
  232.8 6.9 %shard_map.153 = (bf16[8,64,256]{2,1,0:T(8,128)(2,1)}, f32[8,64,256]{2,1,0:T(8,128)S(1)}, f32[8,1,256]{2,1,0:T(1,128)S(1)}) custom-call(bf16[8,3,64,256]{3,2,1,0:T(8,128)(2,1)S(1)} %all-to-all-done.7.packed, f32[16,2048]{1,0:T(8,128)S(1)} %pad_maximum_fusion.6.table, s32[1,2048]{1,0:T(1,128)S(1)} %get-tuple-element.95.starts), custom_call_target="tpu_custom_call" | custom-call | flops 1073741824 | bytes 2097152 | tf_op jit(solution)/shard_map/pallas_call | solution.py:85
  239.8 5.9 %all-to-all-start.8 = ((bf16[8,64,256]{2,1,0:T(8,128)(2,1)}), bf16[8,64,256]{2,1,0:T(8,128)(2,1)S(1)}, u32[]{:S(2)}, u32[]{:S(2)}) async-start(bf16[8,64,256]{2,1,0:T(8,128)(2,1)} %get-tuple-element.15), calls=%async_computation.8 | async-start | bytes 524288 | tf_op jit(solution)/shard_map/all_to_all | solution.py:158
  245.7 7.4 %shard_map.154 = bf16[8,3,64,256]{3,2,1,0:T(8,128)(2,1)} custom-call(bf16[8,3,64,256]{3,2,1,0:T(8,128)(2,1)S(1)} %all-to-all-done.7.packed, f32[16,2048]{1,0:T(8,128)S(1)} %pad_maximum_fusion.6.table, s32[1,2048]{1,0:T(1,128)S(1)} %get-tuple-element.95.starts, f32[8,64,256]{2,1,0:T(8,128)S(1)} %get-tuple-element.16.wide, ...), custom_call_target="tpu_custom_call" | custom-call | flops 2684354560 | bytes 4194304 | tf_op jit(solution)/shard_map/pallas_call | solution.py:140
  257.3 6.5 %all_to_all.152 = bf16[2,4,4,32,1024]{4,3,1,2,0:T(8,128)(2,1)} all-to-all(bf16[2,4,4,32,1024]{4,3,1,2,0:T(8,128)(2,1)S(1)} %bitcast.302), channel_id=1, replica_groups={{0,1},{2,3},{4,5},{6,7},{8,9},{10,11},{12,13},{14,15},{16,17},{18,19},{..., dimensions={0} | all-to-all | bytes 4194304 | tf_op jit(solution)/shard_map/all_to_all | solution.py:158
  263.7 6.0 %all-to-all-start.16 = ((bf16[8,3,64,256]{3,2,1,0:T(8,128)(2,1)}), bf16[8,3,64,256]{3,2,1,0:T(8,128)(2,1)}, u32[]{:S(2)}, u32[]{:S(2)}) async-start(bf16[8,3,64,256]{3,2,1,0:T(8,128)(2,1)} %shard_map.154), calls=%async_computation.16 | async-start | bytes 1572864 | tf_op jit(solution)/shard_map/all_to_all | solution.py:158
  269.7 5.2 convert_reduce_fusion.3
  276.8 5.2 all-to-all-done.16
  287.2 5.4 all_to_all.153
  292.6 4.2 all-to-all-start.10
  298.8 13.8 %all-to-all-done.10 = bf16[4,4,32,1024]{3,2,1,0:T(8,128)(2,1)} async-done(((bf16[4,4,32,1024]{3,2,1,0:T(8,128)(2,1)}), bf16[4,4,32,1024]{3,2,1,0:T(8,128)(2,1)}, u32[]{:S(2)}, u32[]{:S(2)}) %all-to-all-start.10) | async-done | bytes 1048608 | tf_op jit(solution)/shard_map/all_to_all | solution.py:158
  312.6 4.3 all-to-all-start.18
  316.9 4.7 copy.252
  326.9 4.9 all-to-all-done.18
  352.0 10.1 %all-to-all-done.19 = bf16[4,128,1024]{2,1,0:T(8,128)(2,1)S(1)} async-done(((bf16[4,128,1024]{2,1,0:T(8,128)(2,1)}), bf16[4,128,1024]{2,1,0:T(8,128)(2,1)S(1)}, u32[]{:S(2)}, u32[]{:S(2)}) %all-to-all-start.19) | async-done | bytes 1048608 | tf_op jit(solution)/shard_map/all_to_all | solution.py:158
  362.4 5.8 %all_to_all.154 = bf16[2,4,128,1024]{3,2,1,0:T(8,128)(2,1)S(1)} all-to-all(bf16[2,4,128,1024]{3,2,1,0:T(8,128)(2,1)S(1)} %broadcast_in_dim.158), channel_id=1, replica_groups={{0,1},{2,3},{4,5},{6,7},{8,9},{10,11},{12,13},{14,15},{16,17},{18,19},{..., dimensions={0} | all-to-all | bytes 4194304 | tf_op jit(solution)/shard_map/all_to_all | solution.py:158
  378.4 4.3 copy.280
  413.7 4.7 copy.278
  424.5 7.2 %all-to-all-start.21 = ((bf16[64,16,128]{2,1,0:T(8,128)(2,1)}), bf16[64,16,128]{2,1,0:T(8,128)(2,1)S(1)}, u32[]{:S(2)}, u32[]{:S(2)}) async-start(bf16[64,16,128]{2,1,0:T(8,128)(2,1)} %reshape.463), calls=%async_computation.21 | async-start | bytes 524288 | tf_op jit(solution)/shard_map/all_to_all | solution.py:158
  432.5 8.9 %all-to-all-done.21 = bf16[64,16,128]{2,1,0:T(8,128)(2,1)S(1)} async-done(((bf16[64,16,128]{2,1,0:T(8,128)(2,1)}), bf16[64,16,128]{2,1,0:T(8,128)(2,1)S(1)}, u32[]{:S(2)}, u32[]{:S(2)}) %all-to-all-start.21) | async-done | bytes 262176 | tf_op jit(solution)/shard_map/all_to_all | solution.py:158
  441.8 7.5 %shard_map.155 = bf16[8,3,64,256]{3,2,1,0:T(8,128)(2,1)} custom-call(bf16[8,3,64,256]{3,2,1,0:T(8,128)(2,1)S(1)} %all-to-all-done.1.packed, f32[16,2048]{1,0:T(8,128)S(1)} %pad_maximum_fusion.6.table, s32[1,2048]{1,0:T(1,128)S(1)} %get-tuple-element.95.starts, f32[8,64,256]{2,1,0:T(8,128)S(1)} %get-tuple-element.18.wide, ...), custom_call_target="tpu_custom_call" | custom-call | flops 2684354560 | bytes 4194304 | tf_op jit(solution)/shard_map/pallas_call | solution.py:140
  452.9 4.6 fusion.91
  457.6 7.7 %all-to-all-done.22 = bf16[8,3,64,256]{3,2,1,0:T(8,128)(2,1)S(1)} async-done(((bf16[8,3,64,256]{3,2,1,0:T(8,128)(2,1)}), bf16[8,3,64,256]{3,2,1,0:T(8,128)(2,1)S(1)}, u32[]{:S(2)}, u32[]{:S(2)}) %all-to-all-start.22) | async-done | bytes 786464 | tf_op jit(solution)/shard_map/all_to_all | solution.py:158
  480.2 5.9 %fusion.95 = (f32[1024]{0:T(1024)S(1)}, f32[1024]{0:T(1024)S(1)}, f32[1024,1024]{0,1:T(8,128)}) fusion(f32[1024]{0:T(1024)S(1)} %bitcast.355, f32[1024,1024]{0,1:T(8,128)} %copy.274, f32[1024]{0:T(1024)S(1)} %bitcast.358, f32[1024,1024]{0,1:T(8,128)} %fusion.91, f32[1024]{0:T(1024)S(1)} %bitcast.362, f32[1024]{0:T(1024)S(1)} %bitcast.365, ...), kind=kOutput, calls=%fused_computation.228 | convolution fusion | flops 813692928 | bytes 14180352 | tf_op jit(solution)/shard_map/dot_general | solution.py:27
  486.0 4.8 all-to-all-start.27
  490.8 4.7 multiply_convert_fusion
  508.3 6.6 %all_to_all.155 = bf16[2,4,1024,128]{2,3,1,0:T(8,128)(2,1)S(1)} all-to-all(bf16[2,4,1024,128]{2,3,1,0:T(8,128)(2,1)} %bitcast.300), channel_id=1, replica_groups={{0,1},{2,3},{4,5},{6,7},{8,9},{10,11},{12,13},{14,15},{16,17},{18,19},{..., dimensions={0} | all-to-all | bytes 4194304 | tf_op jit(solution)/shard_map/all_to_all | solution.py:158
  515.0 10.2 %all_to_all.156 = f32[8,1,1664]{2,1,0:T(1,128)S(1)} all-to-all(f32[8,1,1664]{2,1,0:T(1,128)S(1)} %broadcast_in_dim.169), channel_id=1, replica_groups=mesh['dp'=2,'seq'=8,'tensor'=8] {'tensor'}, dimensions={0} | all-to-all | bytes 106496 | tf_op jit(solution)/shard_map/all_to_all | solution.py:158
  525.2 5.5 all-to-all-start.25
  532.4 14.3 %all-to-all-done.25 = bf16[16,64,384]{2,1,0:T(8,128)(2,1)S(1)} async-done(((bf16[16,64,384]{2,1,0:T(8,128)(2,1)}), bf16[16,64,384]{2,1,0:T(8,128)(2,1)S(1)}, u32[]{:S(2)}, u32[]{:S(2)}) %all-to-all-start.25) | async-done | bytes 786464 | tf_op jit(solution)/shard_map/all_to_all | solution.py:158
  558.1 5.4 all-to-all-done.24
  (420 shorter events, 227.9 us)
Async XLA Ops:
  7.2 72.3 %all-gather.5.cloned.1.call-start = ((), (), s32[]{:S(2)}) async-start(), calls=%async_computation.31 | async-start | bytes 2228224 | tf_op jit(solution)/shard_map/all_gather | solution.py:239
  8.9 129.4 %all-gather.9.cloned.1.call-start = ((), (), s32[]{:S(2)}) async-start(), calls=%async_computation.33 | async-start | bytes 2113536 | tf_op jit(solution)/shard_map/all_gather | solution.py:242
  11.2 10.0 %copy-start = (bf16[4,256,1024]{2,1,0:T(8,128)(2,1)S(1)}, bf16[4,256,1024]{2,1,0:T(8,128)(2,1)}, u32[]{:S(2)}) copy-start(bf16[4,256,1024]{2,1,0:T(8,128)(2,1)} %param.9) | copy-start | bytes 6291460
  13.2 25.6 %all-to-all-start = ((bf16[16,80,384]{2,1,0:T(8,128)(2,1)}), bf16[16,80,384]{2,1,0:T(8,128)(2,1)S(1)}, u32[]{:S(2)}, u32[]{:S(2)}) async-start(bf16[16,80,384]{2,1,0:T(8,128)(2,1)} %broadcast_in_dim.145), calls=%async_computation | async-start | bytes 1966080 | tf_op jit(solution)/shard_map/all_to_all | solution.py:158
  20.3 181.0 %all-gather.7.cloned.1.call-start = ((), (), s32[]{:S(2)}) async-start(), calls=%async_computation.32 | async-start | bytes 3342336 | tf_op jit(solution)/shard_map/all_gather | solution.py:245
  39.8 13.4 %copy-start.30 = (f32[16,704]{1,0:T(8,128)}, f32[16,704]{1,0:T(8,128)S(1)}, u32[]{:S(2)}) copy-start(f32[16,704]{1,0:T(8,128)S(1)} %get-tuple-element.87) | copy-start | bytes 135172
  40.6 13.3 %copy-start.55 = (f32[8,1,128]{2,1,0:T(1,128)}, f32[8,1,128]{2,1,0:T(1,128)S(1)}, u32[]{:S(2)}) copy-start(f32[8,1,128]{2,1,0:T(1,128)S(1)} %get-tuple-element.113) | copy-start | bytes 12292
  46.3 6.8 %copy-start.44 = (f32[8,2048]{1,0:T(8,128)S(1)}, f32[8,2048]{1,0:T(8,128)}, u32[]{:S(2)}) copy-start(f32[8,2048]{1,0:T(8,128)} %get-tuple-element.131) | copy-start | bytes 196612
  49.4 19.1 %all-to-all-start.1 = ((bf16[8,3,64,256]{3,2,1,0:T(8,128)(2,1)}), bf16[8,3,64,256]{3,2,1,0:T(8,128)(2,1)S(1)}, u32[]{:S(2)}, u32[]{:S(2)}) async-start(bf16[8,3,64,256]{3,2,1,0:T(8,128)(2,1)} %bitcast.311), calls=%async_computation.1 | async-start | bytes 1572864 | tf_op jit(solution)/shard_map/all_to_all | solution.py:158
  92.1 17.7 %all-to-all-start.2 = ((bf16[64,16,128]{2,1,0:T(8,128)(2,1)}), bf16[64,16,128]{2,1,0:T(8,128)(2,1)}, u32[]{:S(2)}, u32[]{:S(2)}) async-start(bf16[64,16,128]{2,1,0:T(8,128)(2,1)} %reshape.441), calls=%async_computation.2 | async-start | bytes 524288 | tf_op jit(solution)/shard_map/all_to_all | solution.py:158
  109.8 31.8 %all-to-all-start.4 = ((bf16[4,4,32,1024]{3,2,1,0:T(8,128)(2,1)}), bf16[4,4,32,1024]{3,2,1,0:T(8,128)(2,1)}, u32[]{:S(2)}, u32[]{:S(2)}) async-start(bf16[4,4,32,1024]{3,2,1,0:T(8,128)(2,1)} %copy.239), calls=%async_computation.4 | async-start | bytes 2097152 | tf_op jit(solution)/shard_map/all_to_all | solution.py:158
  141.6 8.1 %copy-start.11 = (bf16[16,8,64,128]{3,1,2,0:T(8,128)(2,1)}, bf16[16,8,64,128]{3,1,2,0:T(8,128)(2,1)S(1)}, u32[]{:S(2)}) copy-start(bf16[16,8,64,128]{3,1,2,0:T(8,128)(2,1)S(1)} %copy.235) | copy-start | bytes 6291460
  143.9 20.1 %all-to-all-start.13 = ((bf16[4,1024,128]{1,2,0:T(8,128)(2,1)}), bf16[4,1024,128]{1,2,0:T(8,128)(2,1)}, u32[]{:S(2)}, u32[]{:S(2)}) async-start(bf16[4,1024,128]{1,2,0:T(8,128)(2,1)} %broadcast_in_dim.155), calls=%async_computation.13 | async-start | bytes 2097152 | tf_op jit(solution)/shard_map/all_to_all | solution.py:158
  151.7 13.4 %copy-start.69 = (f32[128]{0:T(128)}, f32[128]{0:T(128)S(1)}, u32[]{:S(2)}) copy-start(f32[128]{0:T(128)S(1)} %broadcast_multiply_fusion.5) | copy-start | bytes 1540
  152.4 12.7 %copy-start.70 = (f32[128]{0:T(128)}, f32[128]{0:T(128)S(1)}, u32[]{:S(2)}) copy-start(f32[128]{0:T(128)S(1)} %add_rsqrt_fusion.1) | copy-start | bytes 1540
  152.4 16.2 %copy-start.31 = (f32[16,704]{1,0:T(8,128)S(1)}, f32[16,704]{1,0:T(8,128)}, u32[]{:S(2)}) copy-start(f32[16,704]{1,0:T(8,128)} %get-tuple-element.86) | copy-start | bytes 135172
  165.1 18.5 %all-to-all-start.5 = ((bf16[4,128,1024]{2,1,0:T(8,128)(2,1)}), bf16[4,128,1024]{2,1,0:T(8,128)(2,1)S(1)}, u32[]{:S(2)}, u32[]{:S(2)}) async-start(bf16[4,128,1024]{2,1,0:T(8,128)(2,1)} %broadcast_in_dim.151), calls=%async_computation.5 | async-start | bytes 2097152 | tf_op jit(solution)/shard_map/all_to_all | solution.py:158
  189.3 8.4 %copy-start.1 = (bf16[2,4,128,1024]{3,2,1,0:T(8,128)(2,1)}, bf16[2,4,128,1024]{3,2,1,0:T(8,128)(2,1)S(1)}, u32[]{:S(2)}) copy-start(bf16[2,4,128,1024]{3,2,1,0:T(8,128)(2,1)S(1)} %all_to_all.151) | copy-start | bytes 6291460
  192.8 14.5 %all-to-all-start.14 = ((bf16[2,4,1024,128]{2,3,1,0:T(8,128)(2,1)}), bf16[2,4,1024,128]{2,3,1,0:T(8,128)(2,1)}, u32[]{:S(2)}, u32[]{:S(2)}) async-start(bf16[2,4,1024,128]{2,3,1,0:T(8,128)(2,1)} %broadcast_in_dim.156), calls=%async_computation.14 | async-start | bytes 4194304 | tf_op jit(solution)/shard_map/all_to_all | solution.py:158
  207.3 16.4 %all-to-all-start.7 = ((bf16[8,3,64,256]{3,2,1,0:T(8,128)(2,1)}), bf16[8,3,64,256]{3,2,1,0:T(8,128)(2,1)S(1)}, u32[]{:S(2)}, u32[]{:S(2)}) async-start(bf16[8,3,64,256]{3,2,1,0:T(8,128)(2,1)} %bitcast.30), calls=%async_computation.7 | async-start | bytes 1572864 | tf_op jit(solution)/shard_map/all_to_all | solution.py:158
  214.1 13.7 %copy-start.80 = (f32[1,512]{1,0:T(1,128)}, f32[1,512]{1,0:T(1,128)S(1)}, u32[]{:S(2)}) copy-start(f32[1,512]{1,0:T(1,128)S(1)} %constant_dynamic-slice_fusion.1) | copy-start | bytes 6148
  223.7 16.0 %all-to-all-start.15 = ((bf16[8,64,256]{2,1,0:T(8,128)(2,1)}), bf16[8,64,256]{2,1,0:T(8,128)(2,1)S(1)}, u32[]{:S(2)}, u32[]{:S(2)}) async-start(bf16[8,64,256]{2,1,0:T(8,128)(2,1)} %bitcast.48), calls=%async_computation.15 | async-start | bytes 524288 | tf_op jit(solution)/shard_map/all_to_all | solution.py:158
  239.8 13.3 %all-to-all-start.8 = ((bf16[8,64,256]{2,1,0:T(8,128)(2,1)}), bf16[8,64,256]{2,1,0:T(8,128)(2,1)S(1)}, u32[]{:S(2)}, u32[]{:S(2)}) async-start(bf16[8,64,256]{2,1,0:T(8,128)(2,1)} %get-tuple-element.15), calls=%async_computation.8 | async-start | bytes 524288 | tf_op jit(solution)/shard_map/all_to_all | solution.py:158
  257.2 12.4 %copy-start.3 = (bf16[2,4,1024,128]{2,3,0,1:T(8,128)(2,1)S(1)}, bf16[2,4,1024,128]{2,3,0,1:T(8,128)(2,1)}, u32[]{:S(2)}) copy-start(bf16[2,4,1024,128]{2,3,0,1:T(8,128)(2,1)} %copy.251) | copy-start | bytes 6291460
  263.7 18.3 %all-to-all-start.16 = ((bf16[8,3,64,256]{3,2,1,0:T(8,128)(2,1)}), bf16[8,3,64,256]{3,2,1,0:T(8,128)(2,1)}, u32[]{:S(2)}, u32[]{:S(2)}) async-start(bf16[8,3,64,256]{3,2,1,0:T(8,128)(2,1)} %shard_map.154), calls=%async_computation.16 | async-start | bytes 1572864 | tf_op jit(solution)/shard_map/all_to_all | solution.py:158
  292.6 20.0 %all-to-all-start.10 = ((bf16[4,4,32,1024]{3,2,1,0:T(8,128)(2,1)}), bf16[4,4,32,1024]{3,2,1,0:T(8,128)(2,1)}, u32[]{:S(2)}, u32[]{:S(2)}) async-start(bf16[4,4,32,1024]{3,2,1,0:T(8,128)(2,1)} %copy.248), calls=%async_computation.10 | async-start | bytes 2097152 | tf_op jit(solution)/shard_map/all_to_all | solution.py:158
  312.6 19.2 %all-to-all-start.18 = ((bf16[4,4,32,1024]{3,2,1,0:T(8,128)(2,1)}), bf16[4,4,32,1024]{3,2,1,0:T(8,128)(2,1)}, u32[]{:S(2)}, u32[]{:S(2)}) async-start(bf16[4,4,32,1024]{3,2,1,0:T(8,128)(2,1)} %copy.257), calls=%async_computation.18 | async-start | bytes 2097152 | tf_op jit(solution)/shard_map/all_to_all | solution.py:158
  324.3 15.1 %copy-start.6 = (f32[128,1024]{1,0:T(8,128)S(1)}, f32[128,1024]{1,0:T(8,128)}, u32[]{:S(2)}) copy-start(f32[128,1024]{1,0:T(8,128)} %copy-done.5) | copy-start | bytes 1572868
  331.8 11.3 %all-to-all-start.26 = ((bf16[8,64,256]{2,1,0:T(8,128)(2,1)}), bf16[8,64,256]{2,1,0:T(8,128)(2,1)}, u32[]{:S(2)}, u32[]{:S(2)}) async-start(bf16[8,64,256]{2,1,0:T(8,128)(2,1)} %get-tuple-element.14), calls=%async_computation.26 | async-start | bytes 524288 | tf_op jit(solution)/shard_map/all_to_all | solution.py:158
  345.1 17.0 %all-to-all-start.19 = ((bf16[4,128,1024]{2,1,0:T(8,128)(2,1)}), bf16[4,128,1024]{2,1,0:T(8,128)(2,1)S(1)}, u32[]{:S(2)}, u32[]{:S(2)}) async-start(bf16[4,128,1024]{2,1,0:T(8,128)(2,1)} %broadcast_in_dim.157), calls=%async_computation.19 | async-start | bytes 2097152 | tf_op jit(solution)/shard_map/all_to_all | solution.py:158
  348.7 216.1 %reduce-scatter.9.cloned.1.call-start = ((), (), s32[]{:S(2)}) async-start(), calls=%async_computation.35 | async-start | bytes 2506752
  382.7 183.3 %reduce-scatter.7.cloned.1.call-start = ((), (), s32[]{:S(2)}) async-start(), calls=%async_computation.34 | async-start | bytes 3342336
  422.0 9.7 %copy-start.47 = (f32[8,1,128]{2,1,0:T(1,128)S(1)}, f32[8,1,128]{2,1,0:T(1,128)}, u32[]{:S(2)}) copy-start(f32[8,1,128]{2,1,0:T(1,128)} %get-tuple-element.115) | copy-start | bytes 12292
  422.0 9.7 %copy-start.50 = (f32[8,1,128]{2,1,0:T(1,128)S(1)}, f32[8,1,128]{2,1,0:T(1,128)}, u32[]{:S(2)}) copy-start(f32[8,1,128]{2,1,0:T(1,128)} %get-tuple-element.112) | copy-start | bytes 12292
  422.0 9.7 %copy-start.65 = (f32[1024]{0:T(1024)S(1)}, f32[1024]{0:T(1024)}, u32[]{:S(2)}) copy-start(f32[1024]{0:T(1024)} %get-tuple-element.79) | copy-start | bytes 12292
  422.0 9.7 %copy-start.66 = (f32[1024]{0:T(1024)S(1)}, f32[1024]{0:T(1024)}, u32[]{:S(2)}) copy-start(f32[1024]{0:T(1024)} %get-tuple-element.85) | copy-start | bytes 12292
  422.0 9.7 %copy-start.72 = (f32[1024]{0:T(1024)S(1)}, f32[1024]{0:T(1024)}, u32[]{:S(2)}) copy-start(f32[1024]{0:T(1024)} %get-tuple-element.78) | copy-start | bytes 12292
  422.1 9.7 %copy-start.73 = (f32[1024]{0:T(1024)S(1)}, f32[1024]{0:T(1024)}, u32[]{:S(2)}) copy-start(f32[1024]{0:T(1024)} %get-tuple-element.84) | copy-start | bytes 12292
  424.5 16.9 %all-to-all-start.21 = ((bf16[64,16,128]{2,1,0:T(8,128)(2,1)}), bf16[64,16,128]{2,1,0:T(8,128)(2,1)S(1)}, u32[]{:S(2)}, u32[]{:S(2)}) async-start(bf16[64,16,128]{2,1,0:T(8,128)(2,1)} %reshape.463), calls=%async_computation.21 | async-start | bytes 524288 | tf_op jit(solution)/shard_map/all_to_all | solution.py:158
  441.8 11.0 %copy-start.29 = (bf16[1024,512]{1,0:T(8,128)(2,1)S(1)}, bf16[1024,512]{1,0:T(8,128)(2,1)}, u32[]{:S(2)}) copy-start(bf16[1024,512]{1,0:T(8,128)(2,1)} %copy-done.28) | copy-start | bytes 3145732
  449.3 16.0 %all-to-all-start.22 = ((bf16[8,3,64,256]{3,2,1,0:T(8,128)(2,1)}), bf16[8,3,64,256]{3,2,1,0:T(8,128)(2,1)S(1)}, u32[]{:S(2)}, u32[]{:S(2)}) async-start(bf16[8,3,64,256]{3,2,1,0:T(8,128)(2,1)} %shard_map.155), calls=%async_computation.22 | async-start | bytes 1572864 | tf_op jit(solution)/shard_map/all_to_all | solution.py:158
  452.9 12.4 %copy-start.35 = (bf16[128,1024]{1,0:T(8,128)(2,1)S(1)}, bf16[128,1024]{1,0:T(8,128)(2,1)}, u32[]{:S(2)}) copy-start(bf16[128,1024]{1,0:T(8,128)(2,1)} %get-tuple-element.107) | copy-start | bytes 786436
  466.4 19.6 %all-to-all-start.11 = ((bf16[4,128,1024]{2,1,0:T(8,128)(2,1)}), bf16[4,128,1024]{2,1,0:T(8,128)(2,1)S(1)}, u32[]{:S(2)}, u32[]{:S(2)}) async-start(bf16[4,128,1024]{2,1,0:T(8,128)(2,1)} %broadcast_in_dim.153), calls=%async_computation.11 | async-start | bytes 2097152 | tf_op jit(solution)/shard_map/all_to_all | solution.py:158
  486.0 12.7 %all-to-all-start.27 = ((f32[16,1,1664]{2,1,0:T(1,128)}), f32[16,1,1664]{2,1,0:T(1,128)S(1)}, u32[]{:S(2)}, u32[]{:S(2)}) async-start(f32[16,1,1664]{2,1,0:T(1,128)} %all_to_all.118), calls=%async_computation.27 | async-start | bytes 212992 | tf_op jit(solution)/shard_map/all_to_all | solution.py:158
  500.4 6.6 %all-to-all-start.12 = ((bf16[2,4,128,1024]{3,2,1,0:T(8,128)(2,1)}), bf16[2,4,128,1024]{3,2,1,0:T(8,128)(2,1)S(1)}, u32[]{:S(2)}, u32[]{:S(2)}) async-start(bf16[2,4,128,1024]{3,2,1,0:T(8,128)(2,1)} %broadcast_in_dim.154), calls=%async_computation.12 | async-start | bytes 4194304 | tf_op jit(solution)/shard_map/all_to_all | solution.py:158
  525.2 21.6 %all-to-all-start.25 = ((bf16[16,64,384]{2,1,0:T(8,128)(2,1)}), bf16[16,64,384]{2,1,0:T(8,128)(2,1)S(1)}, u32[]{:S(2)}, u32[]{:S(2)}) async-start(bf16[16,64,384]{2,1,0:T(8,128)(2,1)} %bitcast.335), calls=%async_computation.25 | async-start | bytes 1572864 | tf_op jit(solution)/shard_map/all_to_all | solution.py:158
  532.4 21.5 %copy-start.14 = (bf16[2,4,128,1024]{3,2,1,0:T(8,128)(2,1)S(1)}, bf16[2,4,128,1024]{3,2,1,0:T(8,128)(2,1)}, u32[]{:S(2)}) copy-start(bf16[2,4,128,1024]{3,2,1,0:T(8,128)(2,1)} %copy-done.13) | copy-start | bytes 6291460
  547.6 15.9 %all-to-all-start.24 = ((bf16[4,1024,128]{1,2,0:T(8,128)(2,1)}), bf16[4,1024,128]{1,2,0:T(8,128)(2,1)S(1)}, u32[]{:S(2)}, u32[]{:S(2)}) async-start(bf16[4,1024,128]{1,2,0:T(8,128)(2,1)} %fusion.52), calls=%async_computation.24 | async-start | bytes 2097152 | tf_op jit(solution)/shard_map/all_to_all | solution.py:158
  (65 other events, 191.0 us)
Sparse Core Ops, SparseCore 0:
  10.1 60.7 all-gather.4
  74.1 64.0 all-gather.8
  141.0 45.6 all-gather.6
  382.8 74.3 reduce-scatter.8
  460.4 83.4 reduce-scatter.6
